TPU v7x, 256 devices: a whole 4x4x8 slice. The times are simulated.
256 devices in a mesh: dp: 8 (over x, core), ctx: 32 (over y, z).
Axes of the slice: x: 4, y: 4, z: 8, core: 2. Of those that a mesh axis runs over, the one named last changes fastest.
Arguments:
- queries: bfloat16 [8, 8192, 512], P('dp', 'ctx'), may hold values from -6 to 6
- keys: bfloat16 [8, 8192, 512], P('dp', 'ctx'), may hold values from -6 to 6
- values: bfloat16 [8, 8192, 512], P('dp', 'ctx'), may hold values from -6 to 6
- out_weight: bfloat16 [512, 2048], replicated, may hold values from -0.25 to 0.25
- cotangent: bfloat16 [8, 8192, 2048], P('dp', 'ctx'), may hold values from -6 to 6
- prefix: int32 [8], P('dp'), may hold values from 0 to 64
Outputs:
- mixed: bfloat16 [8, 8192, 2048], P('dp', 'ctx')
- query_grad: float32 [8, 8192, 512], P('dp', 'ctx')
- key_grad: float32 [8, 8192, 512], P('dp', 'ctx')
- value_grad: float32 [8, 8192, 512], P('dp', 'ctx')
- weight_grad: float32 [512, 2048], P(('dp', 'ctx'))
All inputs are finite; a program needn't handle non-finite values.
Results may differ from a plain program's by a relative error of at most 0.029.
Values may be sent and summed in bfloat16 or wider, within the bound.
A program may use at most 128 MiB of HBM per device.

v0:
```python
import jax
import jax.numpy as jnp
from jax import lax
from jax.sharding import PartitionSpec as P

HEADS = 4
HEAD_DIM = 128
BLOCK = 128


def partner(block, axis, bit):
    count = lax.axis_size(axis)
    route = []
    for low in range(count):
        high = low | 1 << bit
        if high != low and high < count:
            route += [(low, high), (high, low)]
    return lax.ppermute(block, axis, route)


def shifted(block, axis, distance):
    devices = range(lax.axis_size(axis))
    route = [(i - distance, i) for i in devices if i - distance in devices]
    return lax.ppermute(block, axis, route)


def extended(cells, sides, width):
    for axis, dim in sides:
        count = lax.axis_size(axis)
        ends = count - 1
        head = lax.slice_in_dim(cells, 0, width, axis=dim)
        tail = lax.slice_in_dim(cells, cells.shape[dim] - width, cells.shape[dim], axis=dim)
        cells = jnp.concatenate(
            [
                lax.ppermute(tail, axis, [(i, (i + 1) % count) for i in range(ends)]),
                cells,
                lax.ppermute(head, axis, [((i + 1) % count, i) for i in range(ends)]),
            ],
            axis=dim,
        )
    return cells


def join_halves(my_part, theirs, upper_half, axis_num):
    low_first = jnp.concatenate([my_part, theirs], axis=axis_num)
    high_first = jnp.concatenate([theirs, my_part], axis=axis_num)
    return jnp.where(upper_half == 1, high_first, low_first)


def group_gather(pieces, axis_num, device_pos):
    level_count = len(pieces)
    pieces = list(pieces)
    for level in range(level_count):
        for bit_num in range(level + 1):
            theirs = partner(pieces[level], "ctx", bit_num)
            pieces[level] = join_halves(pieces[level], theirs, device_pos >> bit_num & 1, axis_num)
    return pieces


def split_half(current, upper_half, axis_num):
    half_len = current.shape[axis_num] // 2
    low_part = lax.slice_in_dim(current, 0, half_len, axis=axis_num)
    high_part = lax.slice_in_dim(current, half_len, 2 * half_len, axis=axis_num)
    keep_part = jnp.where(upper_half == 1, high_part, low_part)
    send_part = jnp.where(upper_half == 1, low_part, high_part)
    return (keep_part, send_part)


def group_reduce(pieces, axis_num, device_pos):
    level_count = len(pieces)
    pieces = list(pieces)
    for level in range(level_count):
        for bit_num in reversed(range(level + 1)):
            keep_part, send_part = split_half(pieces[level], device_pos >> bit_num & 1, axis_num)
            pieces[level] = keep_part + partner(
                send_part.astype(jnp.bfloat16), "ctx", bit_num
            ).astype(send_part.dtype)
    return pieces


def coarse_windows(key_value, device_pos, level_count):
    owned = []
    for level in range(level_count):
        level_ratio = 2 ** (level + 1)
        shaped = key_value.reshape(
            key_value.shape[0],
            key_value.shape[1],
            key_value.shape[2] // level_ratio,
            level_ratio,
            key_value.shape[3],
        )
        owned.append(jnp.mean(shaped, axis=3, dtype=jnp.float32).astype(jnp.bfloat16))
    windows = []
    gathered = group_gather(owned, 2, device_pos)
    for level in range(level_count):
        level_ratio = 2 ** (level + 1)
        left_part = shifted(gathered[level], "ctx", level_ratio)
        right_part = shifted(gathered[level], "ctx", -level_ratio)
        windows.append(jnp.concatenate([left_part, gathered[level], right_part], axis=2))
    return windows


def return_windows(grads, device_pos):
    level_count = len(grads)
    owned = []
    totals = []
    for level in range(level_count):
        level_ratio = 2 ** (level + 1)
        left_part, middle_part, right_part = jnp.split(grads[level], 3, axis=2)
        back_left = shifted(left_part.astype(jnp.bfloat16), "ctx", -level_ratio).astype(
            left_part.dtype
        )
        back_right = shifted(right_part.astype(jnp.bfloat16), "ctx", level_ratio).astype(
            right_part.dtype
        )
        totals.append(middle_part + back_left + back_right)
    owned = group_reduce(totals, 2, device_pos)
    return owned


def attend_masks(device_pos, prefix, tok_len, level_count, seq_len):
    first_row = device_pos * tok_len
    row_pos = first_row + jnp.arange(tok_len, dtype=jnp.int32)
    prefix_end = prefix * BLOCK
    col_pos = first_row - BLOCK + jnp.arange(tok_len + 2 * BLOCK, dtype=jnp.int32)
    nearby = jnp.abs(col_pos[None, :] // BLOCK - row_pos[:, None] // BLOCK) <= 1
    inside = (col_pos >= 0) & (col_pos < seq_len)
    allowed = (col_pos[None, None, :] < prefix_end[:, None, None]) | (
        col_pos[None, None, :] <= row_pos[None, :, None]
    )
    mask_list = [(nearby & inside[None, :])[None] & allowed]
    weight_list = [jnp.ones((tok_len + 2 * BLOCK,), jnp.float32)]
    for level in range(1, level_count + 1):
        level_ratio = 2**level
        parent_idx = device_pos // level_ratio
        own_block = device_pos // (level_ratio // 2)
        entries = (parent_idx - 1) * 2 * BLOCK + jnp.arange(6 * BLOCK, dtype=jnp.int32)
        blocks = entries // BLOCK
        listed = (
            (blocks >= 0)
            & (blocks < seq_len // (BLOCK * level_ratio))
            & (jnp.abs(blocks - own_block) >= 2)
        )
        usable = listed[None, :] & (
            (blocks < own_block)[None, :]
            | (((entries + 1) * level_ratio)[None, :] <= prefix_end[:, None])
        )
        mask_list.append(
            jnp.broadcast_to(usable[:, None, :], (prefix.shape[0], tok_len, 6 * BLOCK))
        )
        weight_list.append(jnp.full((6 * BLOCK,), float(level_ratio), jnp.float32))
    return (jnp.concatenate(mask_list, axis=2), jnp.concatenate(weight_list))


def shards(queries, keys, values, out_weight, cotangent, prefix):
    seq_count, tok_len, feat_width = queries.shape
    ctx_count = lax.axis_size("ctx")
    level_count = min(ctx_count.bit_length() - 2, 2)
    seq_len = tok_len * ctx_count
    device_pos = lax.axis_index("ctx")
    score_scale = HEAD_DIM ** (-0.5)
    key_value = jnp.stack([keys, values])
    fine_pair = extended(key_value, (("ctx", 2),), BLOCK)
    windows = coarse_windows(key_value, device_pos, level_count)
    all_pair = jnp.concatenate([fine_pair] + windows, axis=2)
    key_count = all_pair.shape[2]
    key_heads = all_pair[0].reshape(seq_count, key_count, HEADS, HEAD_DIM)
    value_heads = all_pair[1].reshape(seq_count, key_count, HEADS, HEAD_DIM)
    query_heads = queries.reshape(seq_count, tok_len, HEADS, HEAD_DIM)
    live_mask, weights = attend_masks(device_pos, prefix, tok_len, level_count, seq_len)
    is_live = live_mask[:, None]
    scores = (
        jnp.einsum("sthe,skhe->shtk", query_heads, key_heads, preferred_element_type=jnp.float32)
        * score_scale
    )
    row_peak = jnp.max(jnp.where(is_live, scores, -jnp.inf), axis=3, keepdims=True)
    scaled = jnp.where(is_live, jnp.exp(scores - row_peak) * weights, 0.0)
    norm_total = jnp.sum(scaled, axis=3, keepdims=True)
    weighted = scaled.astype(jnp.bfloat16)
    summed = jnp.einsum(
        "shtk,skhe->sthe", weighted, value_heads, preferred_element_type=jnp.float32
    )
    attended_heads = (summed / jnp.transpose(norm_total, (0, 2, 1, 3))).astype(jnp.bfloat16)
    attended = attended_heads.reshape(seq_count, tok_len, feat_width)
    mixed = jnp.einsum(
        "sth,hd->std", attended, out_weight, preferred_element_type=jnp.float32
    ).astype(jnp.bfloat16)
    grad_attended = jnp.einsum(
        "std,hd->sth", cotangent, out_weight, preferred_element_type=jnp.float32
    ).astype(jnp.bfloat16)
    weight_grad = lax.psum_scatter(
        jnp.einsum("sth,std->hd", attended, cotangent, preferred_element_type=jnp.float32),
        ("dp", "ctx"),
        scatter_dimension=0,
        tiled=True,
    )
    back_heads = grad_attended.reshape(seq_count, tok_len, HEADS, HEAD_DIM)
    probability = scaled / norm_total
    prob_half = probability.astype(jnp.bfloat16)
    row_delta = jnp.sum(back_heads.astype(jnp.float32) * attended_heads.astype(jnp.float32), axis=3)
    row_delta = jnp.transpose(row_delta, (0, 2, 1))[:, :, :, None]
    prob_grad = jnp.einsum(
        "sthe,skhe->shtk", back_heads, value_heads, preferred_element_type=jnp.float32
    )
    score_grad = (probability * (prob_grad - row_delta)).astype(jnp.bfloat16)
    query_grad = (
        jnp.einsum("shtk,skhe->sthe", score_grad, key_heads, preferred_element_type=jnp.float32)
        * score_scale
    )
    key_part = (
        jnp.einsum("shtk,sthe->skhe", score_grad, query_heads, preferred_element_type=jnp.float32)
        * score_scale
    )
    value_part = jnp.einsum(
        "shtk,sthe->skhe", prob_half, back_heads, preferred_element_type=jnp.float32
    )
    pair_grad = jnp.stack(
        [
            key_part.reshape(seq_count, key_count, feat_width),
            value_part.reshape(seq_count, key_count, feat_width),
        ]
    )
    fine_span = tok_len + 2 * BLOCK
    fine_grad = pair_grad[:, :, :fine_span]
    own_grad = fine_grad[:, :, BLOCK : BLOCK + tok_len]
    from_prev = shifted(fine_grad[:, :, fine_span - BLOCK :].astype(jnp.bfloat16), "ctx", 1).astype(
        jnp.float32
    )
    from_next = shifted(fine_grad[:, :, :BLOCK].astype(jnp.bfloat16), "ctx", -1).astype(jnp.float32)
    own_grad = own_grad.at[:, :, :BLOCK].add(from_prev).at[:, :, tok_len - BLOCK :].add(from_next)
    level_grads = []
    for level in range(level_count):
        offset = fine_span + level * 6 * BLOCK
        level_grads.append(pair_grad[:, :, offset : offset + 6 * BLOCK])
    owned = return_windows(level_grads, device_pos)
    for level in range(level_count):
        level_ratio = 2 ** (level + 1)
        own_grad = own_grad + jnp.repeat(owned[level], level_ratio, axis=2) / level_ratio
    return (
        mixed,
        query_grad.reshape(seq_count, tok_len, feat_width),
        own_grad[0],
        own_grad[1],
        weight_grad,
    )


def solution(mesh):
    in_specs = (
        P("dp", "ctx", None),
        P("dp", "ctx", None),
        P("dp", "ctx", None),
        P(),
        P("dp", "ctx", None),
        P("dp"),
    )
    out_specs = (
        P("dp", "ctx", None),
        P("dp", "ctx", None),
        P("dp", "ctx", None),
        P("dp", "ctx", None),
        P(("dp", "ctx"), None),
    )
    return jax.shard_map(shards, mesh=mesh, in_specs=in_specs, out_specs=out_specs, check_vma=False)
```

profile of v0, /device:TPU:2, one launch (start us, length us, event | category | flops | bytes accessed | tf_op | source)
XLA Modules:
  0.0 516.7 jit_solution(3768523029472276602)
XLA Ops:
  7.2 2.1 fusion.43
  9.3 4.5 collective-permute-start
  13.9 1.3 collective-permute-start.1
  15.2 1.1 stack.28
  16.2 1.1 stack.27
  17.3 1.4 convert_reduce_fusion.1
  18.7 0.7 fusion.41
  19.4 2.6 collective-permute-start.2
  22.1 1.0 stack.31
  23.2 0.7 convert_reduce_fusion
  23.9 0.7 fusion.88
  24.6 2.7 convolution_convert_fusion.1
  27.2 1.1 copy.80
  28.4 1.8 copy.102
  32.1 1.8 copy.101
  33.9 1.0 fusion.40
  34.9 2.6 add_bitcast_fusion
  37.6 1.1 maximum_select_fusion.2
  38.6 3.8 collective-permute-start.6
  42.4 1.3 maximum_select_fusion
  43.7 2.0 collective-permute-start.3
  45.8 1.3 collective-permute-start.4
  47.1 1.0 constant_dynamic-update-slice_fusion.7
  48.0 18.3 %collective-permute-done.6 = bf16[2,1,128,512]{3,2,0,1:T(8,128)(2,1)S(1)} collective-permute-done((bf16[2,1,128,512]{3,2,0,1:T(8,128)(2,1)S(1)}, bf16[2,1,128,512]{3,2,0,1:T(8,128)(2,1)S(1)}, u32[]{:S(2)}, u32[]{:S(2)}) %collective-permute-start.6) | collective-permute-done | bytes 262176 | tf_op jit(solution)/shard_map/ppermute | solution.py:18
  66.5 6.7 %collective-permute-start.7 = (bf16[2,1,256,512]{3,2,0,1:T(8,128)(2,1)S(1)}, bf16[2,1,256,512]{3,2,0,1:T(8,128)(2,1)S(1)}, u32[]{:S(2)}, u32[]{:S(2)}) collective-permute-start(bf16[2,1,256,512]{3,2,0,1:T(8,128)(2,1)S(1)} %maximum_select_fusion.1), channel_id=1, source_target_pairs={{0,4},{1,5},{2,6},{3,7},{4,8},{5,9},{6,10},{7,11},{8,12},{9,13},{1... | collective-permute-start | bytes 1572872 | tf_op jit(solution)/shard_map/ppermute | solution.py:24
  73.3 1.0 constant_dynamic-update-slice_fusion.6
  74.2 1.5 collective-permute-start.8
  76.5 8.0 %collective-permute-done.7 = bf16[2,1,256,512]{3,2,0,1:T(8,128)(2,1)S(1)} collective-permute-done((bf16[2,1,256,512]{3,2,0,1:T(8,128)(2,1)S(1)}, bf16[2,1,256,512]{3,2,0,1:T(8,128)(2,1)S(1)}, u32[]{:S(2)}, u32[]{:S(2)}) %collective-permute-start.7) | collective-permute-done | bytes 524320 | tf_op jit(solution)/shard_map/ppermute | solution.py:24
  84.6 23.9 %collective-permute-done.8 = bf16[2,1,256,512]{3,2,0,1:T(8,128)(2,1)S(1)} collective-permute-done((bf16[2,1,256,512]{3,2,0,1:T(8,128)(2,1)S(1)}, bf16[2,1,256,512]{3,2,0,1:T(8,128)(2,1)S(1)}, u32[]{:S(2)}, u32[]{:S(2)}) %collective-permute-start.8) | collective-permute-done | bytes 524320 | tf_op jit(solution)/shard_map/ppermute | solution.py:24
  108.6 2.3 fusion.70
  110.8 4.0 copy.74
  114.9 3.9 copy.73
  118.8 10.1 %fusion.71 = (f32[4,256]{1,0:T(4,128)S(1)}, f32[4,256,2048]{1,2,0:T(8,128)}) fusion(f32[2048]{0:T(1024)S(1)} %copy-done.12, pred[256,2048]{0,1:T(8,128)(4,1)S(1)} %copy-done.10, bf16[2048,4,128]{0,2,1:T(8,128)(2,1)} %bitcast.103, bf16[256,4,128]{0,2,1:T(8,128)(2,1)S(1)} %bitcast.118), kind=kOutput, calls=%fused_computation.144 | convolution fusion | flops 1088423936 | bytes 11284480 | tf_op jit(solution)/shard_map/sub | solution.py:177
  128.9 4.9 multiply_reduce_fusion
  133.9 2.1 copy-done.5
  136.0 1.6 multiply_convert_fusion
  137.6 0.7 convolution_multiply_fusion.1
  138.6 3.5 convolution_multiply_fusion
  142.1 3.5 fusion.7
  145.6 5.3 %copy.87 = f32[1,1,2048,512]{3,2,0,1:T(8,128)} copy(f32[1,1,2048,512]{2,3,1,0:T(8,128)} %bitcast.102) | data formatting | bytes 8388608 | tf_op jit(solution)/shard_map/stack;reshape | solution.py:217
  150.9 5.5 %copy.88 = f32[1,1,2048,512]{3,2,0,1:T(8,128)} copy(f32[1,1,2048,512]{2,3,1,0:T(8,128)} %bitcast.107) | data formatting | bytes 8388608 | tf_op jit(solution)/shard_map/stack;reshape | solution.py:217
  156.4 4.2 fusion.1
  160.5 1.2 fusion.68
  161.7 0.9 fusion.69
  162.6 1.0 copy.93
  163.6 20.0 %collective-permute-start.12 = (bf16[2,1,256,512]{3,2,0,1:T(8,128)(2,1)}, bf16[2,1,256,512]{3,2,0,1:T(8,128)(2,1)S(1)}, u32[]{:S(2)}, u32[]{:S(2)}) collective-permute-start(bf16[2,1,256,512]{3,2,0,1:T(8,128)(2,1)} %get-tuple-element.55), channel_id=1, source_target_pairs={{0,2},{1,3},{2,4},{3,5},{4,6},{5,7},{6,8},{7,9},{8,10},{9,11},{10,... | collective-permute-start | bytes 1572872 | tf_op jit(solution)/shard_map/ppermute | solution.py:24
  183.6 1.3 collective-permute-start.11
  184.9 6.9 %collective-permute-start.15 = (bf16[2,1,256,512]{3,2,0,1:T(8,128)(2,1)}, bf16[2,1,256,512]{3,2,0,1:T(8,128)(2,1)}, u32[]{:S(2)}, u32[]{:S(2)}) collective-permute-start(bf16[2,1,256,512]{3,2,0,1:T(8,128)(2,1)} %get-tuple-element.53), channel_id=1, source_target_pairs={{0,4},{1,5},{2,6},{3,7},{4,8},{5,9},{6,10},{7,11},{8,12},{9,13},{1... | collective-permute-start | bytes 1572872 | tf_op jit(solution)/shard_map/ppermute | solution.py:24
  191.8 1.3 collective-permute-start.14
  193.1 7.9 %collective-permute-start.9 = (bf16[2,1,128,512]{3,2,0,1:T(8,128)(2,1)}, bf16[2,1,128,512]{3,2,0,1:T(8,128)(2,1)}, u32[]{:S(2)}, u32[]{:S(2)}) collective-permute-start(bf16[2,1,128,512]{3,2,0,1:T(8,128)(2,1)} %get-tuple-element.57), channel_id=1, source_target_pairs={{0,1},{1,2},{2,3},{3,4},{4,5},{5,6},{6,7},{7,8},{8,9},{9,10},{10,1... | collective-permute-start | bytes 786440 | tf_op jit(solution)/shard_map/ppermute | solution.py:24
  201.0 3.9 fusion.31
  204.9 1.7 fusion.14
  206.6 1.3 collective-permute-start.10
  207.9 29.8 %collective-permute-done.11 = bf16[2,1,256,512]{3,2,0,1:T(8,128)(2,1)} collective-permute-done((bf16[2,1,256,512]{3,2,0,1:T(8,128)(2,1)}, bf16[2,1,256,512]{3,2,0,1:T(8,128)(2,1)}, u32[]{:S(2)}, u32[]{:S(2)}) %collective-permute-start.11) | collective-permute-done | bytes 524320 | tf_op jit(solution)/shard_map/ppermute | solution.py:24
  237.7 8.7 %collective-permute-done.14 = bf16[2,1,256,512]{3,2,0,1:T(8,128)(2,1)} collective-permute-done((bf16[2,1,256,512]{3,2,0,1:T(8,128)(2,1)S(1)}, bf16[2,1,256,512]{3,2,0,1:T(8,128)(2,1)}, u32[]{:S(2)}, u32[]{:S(2)}) %collective-permute-start.14) | collective-permute-done | bytes 524320 | tf_op jit(solution)/shard_map/ppermute | solution.py:24
  246.4 3.0 fusion.27
  249.5 14.1 %collective-permute-start.16 = (bf16[2,1,128,512]{3,2,0,1:T(8,128)(2,1)S(1)}, bf16[2,1,128,512]{3,2,0,1:T(8,128)(2,1)S(1)}, u32[]{:S(2)}, u32[]{:S(2)}) collective-permute-start(bf16[2,1,128,512]{3,2,0,1:T(8,128)(2,1)S(1)} %select_convert_fusion), channel_id=1, source_target_pairs={{0,2},{2,0},{1,3},{3,1},{4,6},{6,4},{5,7},{7,5},{8,10},{10,8},{9,1... | collective-permute-start | bytes 786440 | tf_op jit(solution)/shard_map/ppermute | solution.py:18
  263.7 12.6 %collective-permute-start.13 = (bf16[2,1,128,512]{3,2,0,1:T(8,128)(2,1)S(1)}, bf16[2,1,128,512]{3,2,0,1:T(8,128)(2,1)S(1)}, u32[]{:S(2)}, u32[]{:S(2)}) collective-permute-start(bf16[2,1,128,512]{3,2,0,1:T(8,128)(2,1)S(1)} %select_convert_fusion.1), channel_id=1, source_target_pairs={{0,1},{1,0},{2,3},{3,2},{4,5},{5,4},{6,7},{7,6},{8,9},{9,8},{10,11... | collective-permute-start | bytes 786440 | tf_op jit(solution)/shard_map/ppermute | solution.py:18
  276.3 1.0 fusion.38
  277.6 6.7 %collective-permute-start.17 = (bf16[2,1,64,512]{3,2,0,1:T(8,128)(2,1)S(1)}, bf16[2,1,64,512]{3,2,0,1:T(8,128)(2,1)S(1)}, u32[]{:S(2)}, u32[]{:S(2)}) collective-permute-start(bf16[2,1,64,512]{3,2,0,1:T(8,128)(2,1)S(1)} %select_convert_fusion.2), channel_id=1, source_target_pairs={{0,1},{1,0},{2,3},{3,2},{4,5},{5,4},{6,7},{7,6},{8,9},{9,8},{10,11... | collective-permute-start | bytes 393224 | tf_op jit(solution)/shard_map/ppermute | solution.py:18
  284.9 2.9 collective-permute-done.17
  289.1 1.0 slice_bitcast_fusion
  290.1 218.3 %all-reduce.3.cloned.1.call-done = f32[512,2048]{1,0:T(8,128)} async-done(((f32[512,2048]{1,0:T(8,128)}), f32[512,2048]{1,0:T(8,128)}) %all-reduce.3.cloned.1.call-update) | async-done | bytes 4194320
  508.4 1.5 constant_dynamic-slice_fusion
  (69 shorter events, 4.9 us)
Async XLA Ops:
  7.2 17.4 %copy-start = (bf16[512,2048]{1,0:T(8,128)(2,1)S(1)}, bf16[512,2048]{1,0:T(8,128)(2,1)}, u32[]{:S(2)}) copy-start(bf16[512,2048]{1,0:T(8,128)(2,1)} %param.13) | copy-start | bytes 6291460
  7.2 15.9 %copy-start.6 = (bf16[1,256,512]{2,1,0:T(8,128)(2,1)S(1)}, bf16[1,256,512]{2,1,0:T(8,128)(2,1)}, u32[]{:S(2)}) copy-start(bf16[1,256,512]{2,1,0:T(8,128)(2,1)} %param.11) | copy-start | bytes 786436
  7.2 501.2 %all-reduce.3.cloned.1.call-start = ((), (), s32[]{:S(2)}) async-start(), calls=%async_computation | async-start | bytes 8388608
  9.3 37.7 %collective-permute-start = (bf16[2,1,128,512]{3,2,0,1:T(8,128)(2,1)}, bf16[2,1,128,512]{3,2,0,1:T(8,128)(2,1)}, u32[]{:S(2)}, u32[]{:S(2)}) collective-permute-start(bf16[2,1,128,512]{3,2,0,1:T(8,128)(2,1)} %get-tuple-element.63), channel_id=1, source_target_pairs={{0,1},{1,2},{2,3},{3,4},{4,5},{5,6},{6,7},{7,8},{8,9},{9,10},{10,1... | collective-permute-start | bytes 786440 | tf_op jit(solution)/shard_map/ppermute | solution.py:35
  13.9 59.4 %collective-permute-start.1 = (bf16[2,1,128,512]{3,2,0,1:T(8,128)(2,1)}, bf16[2,1,128,512]{3,2,0,1:T(8,128)(2,1)}, u32[]{:S(2)}, u32[]{:S(2)}) collective-permute-start(bf16[2,1,128,512]{3,2,0,1:T(8,128)(2,1)} %get-tuple-element.62), channel_id=1, source_target_pairs={{1,0},{2,1},{3,2},{4,3},{5,4},{6,5},{7,6},{8,7},{9,8},{10,9},{11,1... | collective-permute-start | bytes 786440 | tf_op jit(solution)/shard_map/ppermute | solution.py:37
  19.4 23.0 %collective-permute-start.2 = (bf16[2,1,128,512]{3,2,0,1:T(8,128)(2,1)}, bf16[2,1,128,512]{3,2,0,1:T(8,128)(2,1)}, u32[]{:S(2)}, u32[]{:S(2)}) collective-permute-start(bf16[2,1,128,512]{3,2,0,1:T(8,128)(2,1)} %fusion.41), channel_id=1, source_target_pairs={{0,1},{1,0},{2,3},{3,2},{4,5},{5,4},{6,7},{7,6},{8,9},{9,8},{10,11... | collective-permute-start | bytes 786440 | tf_op jit(solution)/shard_map/ppermute | solution.py:18
  24.6 13.0 %collective-permute-start.5 = (bf16[2,1,64,512]{3,2,0,1:T(8,128)(2,1)}, bf16[2,1,64,512]{3,2,0,1:T(8,128)(2,1)S(1)}, u32[]{:S(2)}, u32[]{:S(2)}) collective-permute-start(bf16[2,1,64,512]{3,2,0,1:T(8,128)(2,1)} %fusion.88), channel_id=1, source_target_pairs={{0,1},{1,0},{2,3},{3,2},{4,5},{5,4},{6,7},{7,6},{8,9},{9,8},{10,11... | collective-permute-start | bytes 393224 | tf_op jit(solution)/shard_map/ppermute | solution.py:18
  27.2 46.0 %copy-start.7 = (bf16[1,256,512]{2,1,0:T(8,128)(2,1)S(1)}, bf16[1,256,512]{2,1,0:T(8,128)(2,1)}, u32[]{:S(2)}) copy-start(bf16[1,256,512]{2,1,0:T(8,128)(2,1)} %param.12) | copy-start | bytes 786436
  38.6 27.7 %collective-permute-start.6 = (bf16[2,1,128,512]{3,2,0,1:T(8,128)(2,1)S(1)}, bf16[2,1,128,512]{3,2,0,1:T(8,128)(2,1)S(1)}, u32[]{:S(2)}, u32[]{:S(2)}) collective-permute-start(bf16[2,1,128,512]{3,2,0,1:T(8,128)(2,1)S(1)} %maximum_select_fusion.2), channel_id=1, source_target_pairs={{0,2},{2,0},{1,3},{3,1},{4,6},{6,4},{5,7},{7,5},{8,10},{10,8},{9,1... | collective-permute-start | bytes 786440 | tf_op jit(solution)/shard_map/ppermute | solution.py:18
  43.7 32.0 %collective-permute-start.3 = (bf16[2,1,256,512]{3,2,0,1:T(8,128)(2,1)S(1)}, bf16[2,1,256,512]{3,2,0,1:T(8,128)(2,1)S(1)}, u32[]{:S(2)}, u32[]{:S(2)}) collective-permute-start(bf16[2,1,256,512]{3,2,0,1:T(8,128)(2,1)S(1)} %maximum_select_fusion), channel_id=1, source_target_pairs={{0,2},{1,3},{2,4},{3,5},{4,6},{5,7},{6,8},{7,9},{8,10},{9,11},{10,... | collective-permute-start | bytes 1572872 | tf_op jit(solution)/shard_map/ppermute | solution.py:24
  45.8 30.7 %collective-permute-start.4 = (bf16[2,1,256,512]{3,2,0,1:T(8,128)(2,1)S(1)}, bf16[2,1,256,512]{3,2,0,1:T(8,128)(2,1)S(1)}, u32[]{:S(2)}, u32[]{:S(2)}) collective-permute-start(bf16[2,1,256,512]{3,2,0,1:T(8,128)(2,1)S(1)} %maximum_select_fusion), channel_id=1, source_target_pairs={{2,0},{3,1},{4,2},{5,3},{6,4},{7,5},{8,6},{9,7},{10,8},{11,9},{12,... | collective-permute-start | bytes 1572872 | tf_op jit(solution)/shard_map/ppermute | solution.py:24
  66.5 17.9 %collective-permute-start.7 = (bf16[2,1,256,512]{3,2,0,1:T(8,128)(2,1)S(1)}, bf16[2,1,256,512]{3,2,0,1:T(8,128)(2,1)S(1)}, u32[]{:S(2)}, u32[]{:S(2)}) collective-permute-start(bf16[2,1,256,512]{3,2,0,1:T(8,128)(2,1)S(1)} %maximum_select_fusion.1), channel_id=1, source_target_pairs={{0,4},{1,5},{2,6},{3,7},{4,8},{5,9},{6,10},{7,11},{8,12},{9,13},{1... | collective-permute-start | bytes 1572872 | tf_op jit(solution)/shard_map/ppermute | solution.py:24
  74.2 34.3 %collective-permute-start.8 = (bf16[2,1,256,512]{3,2,0,1:T(8,128)(2,1)S(1)}, bf16[2,1,256,512]{3,2,0,1:T(8,128)(2,1)S(1)}, u32[]{:S(2)}, u32[]{:S(2)}) collective-permute-start(bf16[2,1,256,512]{3,2,0,1:T(8,128)(2,1)S(1)} %maximum_select_fusion.1), channel_id=1, source_target_pairs={{4,0},{5,1},{6,2},{7,3},{8,4},{9,5},{10,6},{11,7},{12,8},{13,9},{1... | collective-permute-start | bytes 1572872 | tf_op jit(solution)/shard_map/ppermute | solution.py:24
  110.8 8.0 %copy-start.8 = (bf16[1,256,512]{1,2,0:T(8,128)(2,1)S(1)}, bf16[1,256,512]{1,2,0:T(8,128)(2,1)}, u32[]{:S(2)}) copy-start(bf16[1,256,512]{1,2,0:T(8,128)(2,1)} %copy.101) | copy-start | bytes 786436
  110.8 8.0 %copy-start.10 = (pred[256,2048]{0,1:T(8,128)(4,1)S(1)}, pred[256,2048]{0,1:T(8,128)(4,1)}, u32[]{:S(2)}) copy-start(pred[256,2048]{0,1:T(8,128)(4,1)} %add_bitcast_fusion) | copy-start | bytes 1572868
  110.8 8.0 %copy-start.12 = (f32[2048]{0:T(1024)S(1)}, f32[2048]{0:T(1024)}, u32[]{:S(2)}) copy-start(f32[2048]{0:T(1024)} %constant.174.clone.1) | copy-start | bytes 24580
  128.9 4.9 copy-start.4
  128.9 7.0 %copy-start.5 = (f32[4,256,2048]{1,2,0:T(8,128)S(1)}, f32[4,256,2048]{1,2,0:T(8,128)}, u32[]{:S(2)}) copy-start(f32[4,256,2048]{1,2,0:T(8,128)} %get-tuple-element.65) | copy-start | bytes 25165828
  128.9 7.0 %copy-start.11 = (bf16[256,512]{0,1:T(8,128)(2,1)S(1)}, bf16[256,512]{0,1:T(8,128)(2,1)}, u32[]{:S(2)}) copy-start(bf16[256,512]{0,1:T(8,128)(2,1)} %copy.102) | copy-start | bytes 786436
  136.0 1.6 copy-start.3
  137.6 1.0 copy-start.9
  163.6 43.0 %collective-permute-start.12 = (bf16[2,1,256,512]{3,2,0,1:T(8,128)(2,1)}, bf16[2,1,256,512]{3,2,0,1:T(8,128)(2,1)S(1)}, u32[]{:S(2)}, u32[]{:S(2)}) collective-permute-start(bf16[2,1,256,512]{3,2,0,1:T(8,128)(2,1)} %get-tuple-element.55), channel_id=1, source_target_pairs={{0,2},{1,3},{2,4},{3,5},{4,6},{5,7},{6,8},{7,9},{8,10},{9,11},{10,... | collective-permute-start | bytes 1572872 | tf_op jit(solution)/shard_map/ppermute | solution.py:24
  183.6 54.1 %collective-permute-start.11 = (bf16[2,1,256,512]{3,2,0,1:T(8,128)(2,1)}, bf16[2,1,256,512]{3,2,0,1:T(8,128)(2,1)}, u32[]{:S(2)}, u32[]{:S(2)}) collective-permute-start(bf16[2,1,256,512]{3,2,0,1:T(8,128)(2,1)} %get-tuple-element.52), channel_id=1, source_target_pairs={{2,0},{3,1},{4,2},{5,3},{6,4},{7,5},{8,6},{9,7},{10,8},{11,9},{12,... | collective-permute-start | bytes 1572872 | tf_op jit(solution)/shard_map/ppermute | solution.py:24
  184.9 52.8 %collective-permute-start.15 = (bf16[2,1,256,512]{3,2,0,1:T(8,128)(2,1)}, bf16[2,1,256,512]{3,2,0,1:T(8,128)(2,1)}, u32[]{:S(2)}, u32[]{:S(2)}) collective-permute-start(bf16[2,1,256,512]{3,2,0,1:T(8,128)(2,1)} %get-tuple-element.53), channel_id=1, source_target_pairs={{0,4},{1,5},{2,6},{3,7},{4,8},{5,9},{6,10},{7,11},{8,12},{9,13},{1... | collective-permute-start | bytes 1572872 | tf_op jit(solution)/shard_map/ppermute | solution.py:24
  191.8 54.6 %collective-permute-start.14 = (bf16[2,1,256,512]{3,2,0,1:T(8,128)(2,1)S(1)}, bf16[2,1,256,512]{3,2,0,1:T(8,128)(2,1)}, u32[]{:S(2)}, u32[]{:S(2)}) collective-permute-start(bf16[2,1,256,512]{3,2,0,1:T(8,128)(2,1)S(1)} %get-tuple-element.54), channel_id=1, source_target_pairs={{4,0},{5,1},{6,2},{7,3},{8,4},{9,5},{10,6},{11,7},{12,8},{13,9},{1... | collective-permute-start | bytes 1572872 | tf_op jit(solution)/shard_map/ppermute | solution.py:24
  193.1 83.2 %collective-permute-start.9 = (bf16[2,1,128,512]{3,2,0,1:T(8,128)(2,1)}, bf16[2,1,128,512]{3,2,0,1:T(8,128)(2,1)}, u32[]{:S(2)}, u32[]{:S(2)}) collective-permute-start(bf16[2,1,128,512]{3,2,0,1:T(8,128)(2,1)} %get-tuple-element.57), channel_id=1, source_target_pairs={{0,1},{1,2},{2,3},{3,4},{4,5},{5,6},{6,7},{7,8},{8,9},{9,10},{10,1... | collective-permute-start | bytes 786440 | tf_op jit(solution)/shard_map/ppermute | solution.py:24
  206.6 70.7 %collective-permute-start.10 = (bf16[2,1,128,512]{3,2,0,1:T(8,128)(2,1)}, bf16[2,1,128,512]{3,2,0,1:T(8,128)(2,1)S(1)}, u32[]{:S(2)}, u32[]{:S(2)}) collective-permute-start(bf16[2,1,128,512]{3,2,0,1:T(8,128)(2,1)} %get-tuple-element.56), channel_id=1, source_target_pairs={{1,0},{2,1},{3,2},{4,3},{5,4},{6,5},{7,6},{8,7},{9,8},{10,9},{11,1... | collective-permute-start | bytes 786440 | tf_op jit(solution)/shard_map/ppermute | solution.py:24
  246.4 29.9 %copy-start.1 = (f32[1,1,2048,512]{3,2,0,1:T(8,128)S(1)}, f32[1,1,2048,512]{3,2,0,1:T(8,128)}, u32[]{:S(2)}) copy-start(f32[1,1,2048,512]{3,2,0,1:T(8,128)} %copy.87) | copy-start | bytes 12582916
  246.4 29.9 %copy-start.2 = (f32[1,1,2048,512]{3,2,0,1:T(8,128)S(1)}, f32[1,1,2048,512]{3,2,0,1:T(8,128)}, u32[]{:S(2)}) copy-start(f32[1,1,2048,512]{3,2,0,1:T(8,128)} %copy.88) | copy-start | bytes 12582916
  249.5 27.9 %collective-permute-start.16 = (bf16[2,1,128,512]{3,2,0,1:T(8,128)(2,1)S(1)}, bf16[2,1,128,512]{3,2,0,1:T(8,128)(2,1)S(1)}, u32[]{:S(2)}, u32[]{:S(2)}) collective-permute-start(bf16[2,1,128,512]{3,2,0,1:T(8,128)(2,1)S(1)} %select_convert_fusion), channel_id=1, source_target_pairs={{0,2},{2,0},{1,3},{3,1},{4,6},{6,4},{5,7},{7,5},{8,10},{10,8},{9,1... | collective-permute-start | bytes 786440 | tf_op jit(solution)/shard_map/ppermute | solution.py:18
  263.7 20.7 %collective-permute-start.13 = (bf16[2,1,128,512]{3,2,0,1:T(8,128)(2,1)S(1)}, bf16[2,1,128,512]{3,2,0,1:T(8,128)(2,1)S(1)}, u32[]{:S(2)}, u32[]{:S(2)}) collective-permute-start(bf16[2,1,128,512]{3,2,0,1:T(8,128)(2,1)S(1)} %select_convert_fusion.1), channel_id=1, source_target_pairs={{0,1},{1,0},{2,3},{3,2},{4,5},{5,4},{6,7},{7,6},{8,9},{9,8},{10,11... | collective-permute-start | bytes 786440 | tf_op jit(solution)/shard_map/ppermute | solution.py:18
  277.6 10.2 %collective-permute-start.17 = (bf16[2,1,64,512]{3,2,0,1:T(8,128)(2,1)S(1)}, bf16[2,1,64,512]{3,2,0,1:T(8,128)(2,1)S(1)}, u32[]{:S(2)}, u32[]{:S(2)}) collective-permute-start(bf16[2,1,64,512]{3,2,0,1:T(8,128)(2,1)S(1)} %select_convert_fusion.2), channel_id=1, source_target_pairs={{0,1},{1,0},{2,3},{3,2},{4,5},{5,4},{6,7},{7,6},{8,9},{9,8},{10,11... | collective-permute-start | bytes 393224 | tf_op jit(solution)/shard_map/ppermute | solution.py:18
Sparse Core Ops, SparseCore 0:
  205.0 303.3 all-reduce.2
where the time goes:
time: 518 us; the launch traced here: 517 us
  waiting for transfers between devices  311 us (60%)
  starting transfers between devices  95.7 us (18%)
  local copies, waits for them, and re-layouts  40.2 us (8%)
  matrix products  32.7 us (6%)
  other arithmetic  22.4 us (4%)
  between operations  15.1 us (3%)
    unnamed x2, waiting for transfers between devices  218 us
    ppermute x10, waiting for transfers between devices, shifted(): return lax.ppermute(block, axis, route)  71.1 us
    ppermute x10, starting transfers between devices, shifted(): return lax.ppermute(block, axis, route)  50.1 us
    ppermute x6, starting transfers between devices, partner(): return lax.ppermute(block, axis, route)  39.8 us
    ppermute x6, waiting for transfers between devices, partner(): return lax.ppermute(block, axis, route)  21.2 us
    another operation x2, local copies, waits for them, and re-layouts, shards(): jnp.stack([key_part.reshape(seq_count, key_count, feat_width), value_part...  10.8 us
  transfers between devices with their start and end apart: 19, of which 8 were waited for; matrix products, arithmetic and copies ran while one was open for 7% of the time, Pallas kernels for 0%

commit v1 on v0

v1 whole, which is shorter than its diff:
```python
import jax
import jax.numpy as jnp
from jax import lax
from jax.experimental import pallas as pl
from jax.experimental.pallas import tpu as pltpu
from jax.sharding import PartitionSpec as P

HEADS = 4
HEAD_DIM = 128
BLOCK = 128
D = 2048
HD = 512
TOK = 256
LEN = 8192
CTX = 32
KEYS = 1280
SCALE = HEAD_DIM**-0.5
LOG2E = 1.4426950408889634
DEAD = -1e30
MESH = pl.DeviceIdType.MESH
F32 = jnp.float32
BF16 = jnp.bfloat16

PREV, OWN, NEXT, NEAR1, FAR1, THIRD1, NEAR2, FAR2, COPY2 = 0, 1, 3, 4, 5, 6, 7, 8, 9

(
    R_PREV,
    R_NEXT,
    R_NEAR1,
    R_FAR1,
    R_THIRD1,
    R_PAIR,
    R_NEAR2,
    R_FAR2,
    R_COPY2,
    B_PREV,
    B_NEXT,
    B_NEAR1,
    B_FAR1,
    B_THIRD1,
    B_COPY2,
    B_FAR2,
    B_NEAR2,
    B_PAIR,
    B_PIECE,
    W_CORE,
) = range(20)
KINDS = 20
G_PREV, G_NEXT, G_NEAR1, G_FAR1, G_THIRD1, G_COPY2, G_FAR2, G_NEAR2, G_PAIR, G_PIECE = range(10)


def dot(a, b, ca, cb):
    return lax.dot_general(a, b, (((ca,), (cb,)), ((), ())), preferred_element_type=F32)


def slot(index, count=1):
    return pl.ds(index * BLOCK, count * BLOCK)


def kernel(
    prefix_ref,
    q_ref,
    k_ref,
    v_ref,
    w_hbm,
    cot_hbm,
    mixed_hbm,
    dq_ref,
    dk_ref,
    dv_ref,
    dw_ref,
    w_ref,
    cot_ref,
    mixed_ref,
    win,
    co1,
    co2,
    pair2,
    bias,
    go_t,
    att_t,
    keep,
    gsend,
    grecv,
    rs_core_send,
    rs_core_recv,
    rs_x_send,
    rs_x_recv,
    rs_own,
    rs_y_send,
    rs_y_recv,
    rs_z_send,
    rs_z_recv,
    load_sem,
    send_sem,
    recv_sem,
    rs_recv_sem,
):
    dp = lax.axis_index("dp")
    me = lax.axis_index("ctx")
    x, core = lax.div(dp, 2), lax.rem(dp, 2)
    y, z = lax.div(me, 8), lax.rem(me, 8)
    r = lax.rem(me, 4)
    parity = lax.rem(me, 2)
    pi = 1 - 2 * parity
    tau = 1 - 2 * lax.div(r, 2)
    outer = (r == 0) | (r == 3)
    inner = (r == 1) | (r == 2)

    def ctx(offset):
        return (dp, lax.rem(me + offset + 2 * CTX, CTX))

    def row_peer(step):
        return (dp, y * 8 + lax.rem(z + step, 8))

    def column_peer(step):
        return (dp, lax.rem(y + step, 4) * 8 + z)

    sibling = (dp + 1 - 2 * core, me)

    load_w = pltpu.make_async_copy(w_hbm, w_ref, load_sem.at[0])
    load_cot = pltpu.make_async_copy(cot_hbm, cot_ref, load_sem.at[1])
    load_w.start()
    load_cot.start()

    barrier = pltpu.get_barrier_semaphore()
    partners = [ctx(o) for o in (1, -1, 2, -2, 7, -7, 8, -8, 16)]
    partners += [row_peer(s) for s in range(1, 8)]
    partners += [(lax.rem(x + s, 4) * 2 + core, me) for s in range(1, 4)]
    partners += [sibling]
    for partner in partners:
        pl.semaphore_signal(barrier, inc=1, device_id=partner, device_id_type=MESH)

    half = pl.multiple_of(parity * 64, 64)
    other_half = pl.multiple_of(64 - parity * 64, 64)
    entry = lax.broadcasted_iota(jnp.int32, (192, TOK), 0)
    token = lax.broadcasted_iota(jnp.int32, (192, TOK), 1)
    mean1 = (entry < 128) & (lax.shift_right_logical(token, 1) == entry)
    mean2 = (entry >= 128) & (lax.shift_right_logical(token, 2) == entry - 128)
    means = jnp.where(mean1, 0.5, jnp.where(mean2, 0.25, 0.0)).astype(BF16)
    for kv, source in enumerate((k_ref, v_ref)):
        coarse = dot(means, source[...], 1, 0).astype(BF16)
        for h in range(HEADS):
            cols = slice(h * HEAD_DIM, (h + 1) * HEAD_DIM)
            win[h, kv, OWN * BLOCK : (OWN + 2) * BLOCK, :] = source[:, cols]
            co1[h, kv] = coarse[:128, cols]
            co2[h, kv] = coarse[128:, cols]
            pair2[h, kv, pl.ds(half, 64), :] = coarse[128:, cols]

    pl.semaphore_wait(barrier, len(partners))

    started = []

    def send(sems, kind, src, dst, device, when=None):
        send_sems, recv_sems = sems
        copy = pltpu.make_async_remote_copy(
            src_ref=src,
            dst_ref=dst,
            send_sem=send_sems.at[len(started)],
            recv_sem=recv_sems.at[kind],
            device_id=device,
            device_id_type=MESH,
        )
        if when is None:
            copy.start()
        else:
            pl.when(when)(copy.start)
        started.append((when, copy))

    def arrive(sems, kind, dst, device):
        pltpu.make_async_remote_copy(
            src_ref=dst,
            dst_ref=dst,
            send_sem=sems[0].at[0],
            recv_sem=sems[1].at[kind],
            device_id=device,
            device_id_type=MESH,
        ).wait_recv()

    def sems(h):
        return send_sem, recv_sem.at[h]

    def window(h, index):
        return win.at[h, :, slot(index), :]

    def returned(h, index):
        return grecv.at[h, index]

    def first_sends(h):
        piece = pair2.at[h, :, pl.ds(half, 64), :]
        send(sems(h), R_PAIR, piece, piece, ctx(-tau), inner)
        send(sems(h), R_NEAR1, co1.at[h], window(h, NEAR1), ctx(2 * pi))
        send(sems(h), R_FAR1, co1.at[h], window(h, FAR1), ctx(-2 * pi))
        send(sems(h), R_NEXT, window(h, OWN), window(h, NEXT), ctx(-1))
        send(sems(h), R_PREV, window(h, OWN + 1), window(h, PREV), ctx(1))

    def relay_pair(h):
        @pl.when(outer)
        def _():
            arrive(sems(h), R_PAIR, pair2.at[h, :, pl.ds(other_half, 64), :], ctx(tau))

        send(sems(h), R_NEAR2, pair2.at[h], window(h, NEAR2), ctx(7 * tau), outer)

    def relay_near(h):
        arrive(sems(h), R_NEAR2, window(h, NEAR2), ctx(tau))
        send(sems(h), R_NEAR2, window(h, NEAR2), window(h, NEAR2), ctx(tau), outer)
        send(sems(h), R_FAR2, window(h, NEAR2), window(h, FAR2), ctx(tau), inner)
        arrive(sems(h), R_NEAR1, window(h, NEAR1), ctx(2 * pi))
        send(sems(h), R_THIRD1, window(h, NEAR1), window(h, THIRD1), ctx(pi))

    def relay_far(h):
        arrive(sems(h), R_FAR2, window(h, FAR2), ctx(tau))
        send(sems(h), R_FAR2, window(h, FAR2), window(h, FAR2), ctx(-tau), inner)
        send(sems(h), R_COPY2, window(h, FAR2), window(h, COPY2), ctx(-8 * tau))

    def last_arrivals(h):
        arrive(sems(h), R_NEXT, window(h, NEXT), ctx(1))
        arrive(sems(h), R_PREV, window(h, PREV), ctx(-1))
        arrive(sems(h), R_FAR1, window(h, FAR1), ctx(2 * pi))
        arrive(sems(h), R_THIRD1, window(h, THIRD1), ctx(pi))
        arrive(sems(h), R_COPY2, window(h, COPY2), ctx(8 * tau))

    def masks():
        prefix_end = prefix_ref[0] * BLOCK
        first_row = me * TOK
        key = lax.broadcasted_iota(jnp.int32, (4 * BLOCK, TOK), 0)
        query = lax.broadcasted_iota(jnp.int32, (4 * BLOCK, TOK), 1)
        apart = lax.shift_right_logical(key, 7) - lax.shift_right_logical(query, 7)
        column = first_row - BLOCK + key
        live = (apart >= 0) & (apart <= 2) & (column >= 0) & (column < LEN)
        live = live & ((column < prefix_end) | (column <= first_row + query))
        bias[: 4 * BLOCK, :] = jnp.where(live, 0.0, DEAD)
        quad = lax.div(me, 4)
        near2 = jnp.where(tau == 1, 2 * quad + 3, 2 * quad - 2)
        far2 = jnp.where(tau == 1, 2 * quad - 2, 2 * quad + 3)
        copy2 = jnp.where(tau == 1, 2 * quad + 2, 2 * quad - 1)
        level1 = [(NEAR1, me - 2 * pi), (FAR1, me + 2 * pi), (THIRD1, me + 3 * pi)]
        level2 = [(NEAR2, near2), (FAR2, far2), (COPY2, copy2)]
        place = lax.broadcasted_iota(jnp.int32, (BLOCK, TOK), 0)
        for level, entries in ((1, level1), (2, level2)):
            blocks = LEN // (BLOCK << level)
            own = lax.div(me, level)
            for index, block in entries:
                end = (block * BLOCK + place + 1) * (1 << level)
                inside = (block >= 0) & (block < blocks)
                before = jnp.where(inside & (block < own), LEN, 0)
                until = jnp.where(inside, prefix_end, 0)
                usable = (place < before) | ((end <= until) & (end > 0))
                bias[slot(index), :] = jnp.where(usable, float(level), DEAD)

    def attend(h):
        cols = slice(h * HEAD_DIM, (h + 1) * HEAD_DIM)
        key = win[h, 0]
        value = win[h, 1]
        query = q_ref[:, cols]
        scores = dot(key, query, 1, 1) * (SCALE * LOG2E) + bias[...]
        peak = jnp.max(scores, axis=0, keepdims=True)
        weighted = jnp.exp2(scores - peak)
        inverse = 1.0 / jnp.sum(weighted, axis=0, keepdims=True)
        weighted_half = weighted.astype(BF16)
        attended = (dot(value, weighted_half, 0, 0) * inverse).astype(BF16)
        att_t[cols, :] = attended
        back = go_t[cols, :].astype(F32)
        delta = jnp.sum(back * attended.astype(F32), axis=0, keepdims=True) * inverse
        back = (back * inverse).astype(BF16)
        score_grad = (weighted * (dot(value, back, 1, 0) - delta)).astype(BF16)
        dq_ref[:, cols] = jnp.transpose(dot(key, score_grad, 0, 0) * SCALE)
        for kv, grad in enumerate(
            (dot(score_grad, query, 1, 0) * SCALE, dot(weighted_half, back, 1, 1))
        ):
            own = dk_ref if kv == 0 else dv_ref
            own[:, cols] = grad[OWN * BLOCK : (OWN + 2) * BLOCK]
            gsend[h, kv, slot(0), :] = grad[:BLOCK].astype(BF16)
            gsend[h, kv, slot(1), :] = grad[NEXT * BLOCK : (NEXT + 1) * BLOCK].astype(BF16)
            gsend[h, kv, slot(2), :] = grad[FAR1 * BLOCK : (FAR1 + 1) * BLOCK].astype(BF16)
            gsend[h, kv, slot(3), :] = grad[THIRD1 * BLOCK : (THIRD1 + 1) * BLOCK].astype(BF16)
            gsend[h, kv, slot(4), :] = grad[COPY2 * BLOCK :].astype(BF16)
            keep[h, kv, slot(0), :] = grad[NEAR1 * BLOCK : (NEAR1 + 1) * BLOCK]
            keep[h, kv, slot(1), :] = grad[FAR2 * BLOCK : (FAR2 + 1) * BLOCK]
            keep[h, kv, slot(2), :] = grad[NEAR2 * BLOCK : (NEAR2 + 1) * BLOCK]

    def outgoing(h, index):
        return gsend.at[h, :, slot(index), :]

    def back_first(h):
        send(sems(h), B_COPY2, outgoing(h, 4), returned(h, G_COPY2), ctx(8 * tau))
        send(sems(h), B_THIRD1, outgoing(h, 3), returned(h, G_THIRD1), ctx(pi))
        send(sems(h), B_FAR1, outgoing(h, 2), returned(h, G_FAR1), ctx(2 * pi))
        send(sems(h), B_NEXT, outgoing(h, 0), returned(h, G_NEXT), ctx(-1))
        send(sems(h), B_PREV, outgoing(h, 1), returned(h, G_PREV), ctx(1))

    def back_far(h):
        arrive(sems(h), B_COPY2, returned(h, G_COPY2), ctx(-8 * tau))

        @pl.when(inner)
        def _():
            arrive(sems(h), B_FAR2, returned(h, G_FAR2), ctx(-tau))

        theirs = grecv[h, G_COPY2].astype(F32)
        more = jnp.where(inner, grecv[h, G_FAR2].astype(F32), 0.0)
        gsend[h, :, slot(6), :] = (keep[h, :, slot(1), :] + theirs + more).astype(BF16)
        send(sems(h), B_FAR2, outgoing(h, 6), returned(h, G_FAR2), ctx(tau), outer)
        send(sems(h), B_NEAR2, outgoing(h, 6), returned(h, G_NEAR2), ctx(tau), inner)
        arrive(sems(h), B_THIRD1, returned(h, G_THIRD1), ctx(pi))
        theirs = grecv[h, G_THIRD1].astype(F32)
        gsend[h, :, slot(5), :] = (keep[h, :, slot(0), :] + theirs).astype(BF16)
        send(sems(h), B_NEAR1, outgoing(h, 5), returned(h, G_NEAR1), ctx(-2 * pi))

    def back_near(h):
        arrive(sems(h), B_NEAR2, returned(h, G_NEAR2), ctx(tau))
        theirs = grecv[h, G_NEAR2].astype(F32)
        gsend[h, :, slot(7), :] = (keep[h, :, slot(2), :] + theirs).astype(BF16)
        send(sems(h), B_NEAR2, outgoing(h, 7), returned(h, G_NEAR2), ctx(-tau), inner)
        send(sems(h), B_PAIR, outgoing(h, 7), returned(h, G_PAIR), ctx(7 * tau), outer)

    def back_pair(h):
        @pl.when(outer)
        def _():
            arrive(sems(h), B_PAIR, returned(h, G_PAIR), ctx(7 * tau))

        theirs = grecv.at[h, G_PAIR, :, pl.ds(other_half, 64), :]
        mine = grecv.at[h, G_PIECE, :, pl.ds(0, 64), :]
        send(sems(h), B_PIECE, theirs, mine, ctx(tau), outer)

    def finish(h):
        cols = slice(h * HEAD_DIM, (h + 1) * HEAD_DIM)
        arrive(sems(h), B_NEXT, returned(h, G_NEXT), ctx(1))
        arrive(sems(h), B_PREV, returned(h, G_PREV), ctx(-1))
        arrive(sems(h), B_FAR1, returned(h, G_FAR1), ctx(-2 * pi))
        arrive(sems(h), B_NEAR1, returned(h, G_NEAR1), ctx(2 * pi))

        @pl.when(inner)
        def _():
            arrive(sems(h), B_PIECE, grecv.at[h, G_PIECE, :, pl.ds(0, 64), :], ctx(-tau))

        for kv, own in enumerate((dk_ref, dv_ref)):
            level1 = grecv[h, G_FAR1, kv].astype(F32) + grecv[h, G_NEAR1, kv].astype(F32)
            pair = grecv[h, G_PAIR, kv, pl.ds(half, 64), :]
            level2 = jnp.where(outer, pair, grecv[h, G_PIECE, kv, :64, :])
            entries = jnp.concatenate([level1.astype(BF16), level2], axis=0)
            spread = dot(means, entries, 0, 0)
            own[:BLOCK, cols] += spread[:BLOCK] + grecv[h, G_PREV, kv].astype(F32)
            own[BLOCK:, cols] += spread[BLOCK:] + grecv[h, G_NEXT, kv].astype(F32)

    def weight_part(h, which):
        rows = pl.ds(pl.multiple_of(h * HEAD_DIM + which * 64, 64), 64)
        return dot(att_t[rows, :], cot_ref[...], 1, 0)

    def weight_core(h):
        rs_core_send[h] = weight_part(h, 1 - core).astype(BF16)
        send(sems(h), W_CORE, rs_core_send.at[h], rs_core_recv.at[h], sibling)

    rs_sems = (send_sem, rs_recv_sem)

    def weight_x(h):
        arrive(sems(h), W_CORE, rs_core_recv.at[h], sibling)
        total = weight_part(h, core) + rs_core_recv[h].astype(F32)
        rs_x_send[h] = total.astype(BF16)

        @pl.when(x == h)
        def _():
            rs_own[...] = total

        step = lax.rem(x - h + 4, 4)
        place = jnp.maximum(step - 1, 0)
        send(rs_sems, place, rs_x_send.at[h], rs_x_recv.at[place], (h * 2 + core, me), x != h)

    def weight_y():
        for step in range(1, 4):
            device = (lax.rem(x + step, 4) * 2 + core, me)
            arrive(rs_sems, step - 1, rs_x_recv.at[step - 1], device)
        total = rs_own[...]
        for step in range(1, 4):
            total = total + rs_x_recv[step - 1].astype(F32)
        rs_own[...] = total
        rs_y_send[...] = total.astype(BF16)
        for step in range(1, 4):
            rows = pl.ds(pl.multiple_of(lax.rem(y + step, 4) * 16, 16), 16)
            send(rs_sems, 2 + step, rs_y_send.at[rows], rs_y_recv.at[step - 1], column_peer(step))

    def weight_z():
        for step in range(1, 4):
            arrive(rs_sems, 2 + step, rs_y_recv.at[step - 1], column_peer(step))
        total = rs_own[pl.ds(pl.multiple_of(y * 16, 16), 16), :]
        for step in range(1, 4):
            total = total + rs_y_recv[step - 1].astype(F32)
        for part in range(8):
            rs_z_send[part] = total[2 * part : 2 * part + 2]
        for step in range(1, 8):
            part = rs_z_send.at[lax.rem(z + step, 8)]
            send(rs_sems, 5 + step, part, rs_z_recv.at[step - 1], row_peer(step))

    def weight_end():
        for step in range(1, 8):
            arrive(rs_sems, 5 + step, rs_z_recv.at[step - 1], row_peer(step))
        total = rs_z_send[z]
        for step in range(1, 8):
            total = total + rs_z_recv[step - 1]
        dw_ref[...] = total

    for h in range(HEADS):
        first_sends(h)
    masks()
    load_w.wait()
    load_cot.wait()
    go_t[...] = dot(w_ref[...], cot_ref[...], 1, 1).astype(BF16)
    for h in range(HEADS):
        relay_pair(h)
    relay_near(0)
    relay_near(1)
    relay_far(0)
    last_arrivals(0)
    attend(0)
    back_first(0)
    weight_core(0)
    relay_near(2)
    relay_far(1)
    last_arrivals(1)
    attend(1)
    back_first(1)
    weight_core(1)
    relay_near(3)
    relay_far(2)
    back_far(0)
    weight_x(0)
    last_arrivals(2)
    attend(2)
    back_first(2)
    weight_core(2)
    relay_far(3)
    back_far(1)
    back_near(0)
    weight_x(1)
    last_arrivals(3)
    attend(3)
    back_first(3)
    weight_core(3)
    back_far(2)
    back_near(1)
    back_pair(0)
    weight_x(2)
    weight_x(3)
    for part in range(4):
        cols = slice(part * 512, (part + 1) * 512)
        mixed_ref[:, cols] = dot(att_t[...], w_ref[:, cols], 0, 0).astype(BF16)
    store = pltpu.make_async_copy(mixed_ref, mixed_hbm, load_sem.at[2])
    store.start()
    back_far(3)
    back_near(2)
    back_pair(1)
    weight_y()
    back_near(3)
    back_pair(2)
    weight_z()
    finish(0)
    back_pair(3)
    finish(1)
    finish(2)
    weight_end()
    finish(3)
    store.wait()
    for when, copy in started:
        if when is None:
            copy.wait_send()
        else:
            pl.when(when)(copy.wait_send)


SENDS = 112


def shards(queries, keys, values, out_weight, cotangent, prefix):
    vmem = pl.BlockSpec(memory_space=pltpu.VMEM)
    anywhere = pl.BlockSpec(memory_space=pl.ANY)
    pair = (HEADS, 2)
    mixed, dq, dk, dv, dw = pl.pallas_call(
        kernel,
        out_shape=(
            jax.ShapeDtypeStruct((TOK, D), BF16),
            jax.ShapeDtypeStruct((TOK, HD), F32),
            jax.ShapeDtypeStruct((TOK, HD), F32),
            jax.ShapeDtypeStruct((TOK, HD), F32),
            jax.ShapeDtypeStruct((2, D), F32),
        ),
        in_specs=[pl.BlockSpec(memory_space=pltpu.SMEM), vmem, vmem, vmem, anywhere, anywhere],
        out_specs=(anywhere, vmem, vmem, vmem, vmem),
        scratch_shapes=[
            pltpu.VMEM((HD, D), BF16),
            pltpu.VMEM((TOK, D), BF16),
            pltpu.VMEM((TOK, D), BF16),
            pltpu.VMEM(pair + (KEYS, HEAD_DIM), BF16),
            pltpu.VMEM(pair + (128, HEAD_DIM), BF16),
            pltpu.VMEM(pair + (64, HEAD_DIM), BF16),
            pltpu.VMEM(pair + (128, HEAD_DIM), BF16),
            pltpu.VMEM((KEYS, TOK), F32),
            pltpu.VMEM((HD, TOK), BF16),
            pltpu.VMEM((HD, TOK), BF16),
            pltpu.VMEM(pair + (3 * BLOCK, HEAD_DIM), F32),
            pltpu.VMEM(pair + (8 * BLOCK, HEAD_DIM), BF16),
            pltpu.VMEM((HEADS, 10, 2, BLOCK, HEAD_DIM), BF16),
            pltpu.VMEM((HEADS, 64, D), BF16),
            pltpu.VMEM((HEADS, 64, D), BF16),
            pltpu.VMEM((HEADS, 64, D), BF16),
            pltpu.VMEM((3, 64, D), BF16),
            pltpu.VMEM((64, D), F32),
            pltpu.VMEM((64, D), BF16),
            pltpu.VMEM((3, 16, D), BF16),
            pltpu.VMEM((8, 2, D), F32),
            pltpu.VMEM((7, 2, D), F32),
            pltpu.SemaphoreType.DMA((3,)),
            pltpu.SemaphoreType.DMA((SENDS,)),
            pltpu.SemaphoreType.DMA((HEADS, KINDS)),
            pltpu.SemaphoreType.DMA((13,)),
        ],
        compiler_params=pltpu.CompilerParams(
            collective_id=0, has_side_effects=True, vmem_limit_bytes=56 << 20
        ),
        cost_estimate=pl.CostEstimate(
            flops=3_700_000_000, bytes_accessed=8_000_000, transcendentals=1_400_000
        ),
        name="hier_attention",
    )(prefix, queries[0], keys[0], values[0], out_weight, cotangent[0])
    return mixed[None], dq[None], dk[None], dv[None], dw


def solution(mesh):
    tokens = P("dp", "ctx", None)
    return jax.shard_map(
        shards,
        mesh=mesh,
        in_specs=(tokens, tokens, tokens, P(), tokens, P("dp")),
        out_specs=(tokens, tokens, tokens, tokens, P(("dp", "ctx"), None)),
        check_vma=False,
    )
```

time: 518 us -> 139 us (0.27)
  waiting for transfers between devices: 311 us -> 0 us
  Pallas kernels: 0 us -> 130 us
  starting transfers between devices: 95.7 us -> 0 us
  local copies, waits for them, and re-layouts: 40.2 us -> 5.42 us
  matrix products: 32.7 us -> 0 us
  other arithmetic: 22.4 us -> 0 us
  between operations: 15.1 us -> 1.32 us
    unnamed x2 -> x0, waiting for transfers between devices: 218 us -> none
    pallas_call x0 -> x1, Pallas kernels: none -> 130 us  [shards(): pl.pallas_call(kernel, out_shape=(jax.ShapeDtypeStruct((TOK, D), BF16), j...]
    ppermute x18 -> x0, starting transfers between devices: 95.7 us -> none  [the longest x10 50.1 us: shifted(): return lax.ppermute(block, axis, route)]
    ppermute x18 -> x0, waiting for transfers between devices: 92.3 us -> none  [the longest x10 71.1 us: shifted(): return lax.ppermute(block, axis, route)]
    dot_general x8 -> x0, matrix products: 22.6 us -> none  [the longest x1 4.92 us: shards(): jnp.einsum('shtk,skhe->sthe', weighted, value_heads, preferred_element_ty...]
    another operation x8 -> x0, local copies, waits for them, and re-layouts: 17.6 us -> none  [the longest x2 10.8 us: shards(): jnp.stack([key_part.reshape(seq_count, key_count, feat_width), value_part...]
    slice x4 -> x0, local copies, waits for them, and re-layouts: 11.1 us -> none  [the longest x2 6.31 us: shards(): key_heads = all_pair[0].reshape(seq_count, key_count, HEADS, HEAD_DIM)]
    sub x1 -> x0, matrix products: 10.1 us -> none  [shards(): scaled = jnp.where(is_live, jnp.exp(scores - row_peak) * weights, 0.0)]
  transfers between devices with their start and end apart: 19 -> 0, of which waited for: 8 -> 0; matrix products, arithmetic and copies ran while one was open for 7% -> 0% of each run, Pallas kernels for 0% -> 0%
where the time goes in v1:
time: 139 us; the launch traced here: 137 us
  Pallas kernels  130 us (94%)
  local copies, waits for them, and re-layouts  5.42 us (4%)
    pallas_call x1, Pallas kernels, shards(): pl.pallas_call(kernel, out_shape=(jax.ShapeDtypeStruct((TOK, D), BF16), j...  130 us
    unnamed x13, local copies, waits for them, and re-layouts  5.42 us

profile of v1, /device:TPU:2, one launch (start us, length us, event | category | flops | bytes accessed | tf_op | source)
XLA Modules:
  0.0 136.6 jit_solution(3079201825847497249)
XLA Ops:
  1.3 129.8 %hier_attention.1 = (bf16[256,2048]{1,0:T(8,128)(2,1)}, f32[256,512]{1,0:T(8,128)}, f32[256,512]{1,0:T(8,128)}, f32[256,512]{1,0:T(8,128)}, f32[2,2048]{1,0:T(2,128)}) custom-call(s32[1]{0:T(128)S(6)} %copy.16.prefix_ref, bf16[256,512]{1,0:T(8,128)(2,1)} %bitcast.13, bf16[256,512]{1,0:T(8,128)(2,1)} %bitcast.14, bf16[256,512]{1,0:T(8,128)(2,1)} %bitcast.15, ...), custom_call_target="tpu_custom_call" | custom-call | flops 3700000000 | bytes 8000000 | tf_op jit(solution)/shard_map/hier_attention/pallas_call | solution.py:476
  131.1 0.0 copy-start.2
  131.1 0.0 copy-start.1
  131.1 0.0 copy-start
  131.1 2.4 %copy.17 = bf16[1,256,2048]{2,1,0:T(8,128)(2,1)} copy(bf16[1,256,2048]{2,1,0:T(8,128)(2,1)} %bitcast.8) | data formatting | bytes 2097152
  133.6 0.0 copy-done.2
  133.6 0.0 copy-start.3
  133.6 0.8 copy.18
  134.4 0.0 copy-done.1
  134.4 0.8 copy.19
  135.1 0.0 copy-done
  135.2 0.8 copy.20
  135.9 0.0 copy-done.3
  135.9 0.6 copy.21
Async XLA Ops:
  131.1 2.5 %copy-start.2 = (f32[256,512]{1,0:T(8,128)S(1)}, f32[256,512]{1,0:T(8,128)}, u32[]{:S(2)}) copy-start(f32[256,512]{1,0:T(8,128)} %get-tuple-element.11) | copy-start | bytes 1572868
  131.1 3.2 %copy-start.1 = (f32[256,512]{1,0:T(8,128)S(1)}, f32[256,512]{1,0:T(8,128)}, u32[]{:S(2)}) copy-start(f32[256,512]{1,0:T(8,128)} %get-tuple-element.12) | copy-start | bytes 1572868
  131.1 4.0 %copy-start = (f32[256,512]{1,0:T(8,128)S(1)}, f32[256,512]{1,0:T(8,128)}, u32[]{:S(2)}) copy-start(f32[256,512]{1,0:T(8,128)} %get-tuple-element.13) | copy-start | bytes 1572868
  133.6 2.4 %copy-start.3 = (f32[2,2048]{1,0:T(2,128)S(1)}, f32[2,2048]{1,0:T(2,128)}, u32[]{:S(2)}) copy-start(f32[2,2048]{1,0:T(2,128)} %get-tuple-element.24) | copy-start | bytes 49156

commit v2 on v1

--- a/solution.py
+++ b/solution.py
@@ -41,12 +41,11 @@
     B_COPY2,
     B_FAR2,
     B_NEAR2,
-    B_PAIR,
     B_PIECE,
     W_CORE,
-) = range(20)
-KINDS = 20
-G_PREV, G_NEXT, G_NEAR1, G_FAR1, G_THIRD1, G_COPY2, G_FAR2, G_NEAR2, G_PAIR, G_PIECE = range(10)
+) = range(19)
+KINDS = 19
+G_PREV, G_NEXT, G_NEAR1, G_FAR1, G_THIRD1, G_COPY2, G_FAR2, G_NEAR2 = range(8)
 
 
 def dot(a, b, ca, cb):
@@ -59,9 +58,9 @@
 
 def kernel(
     prefix_ref,
-    q_ref,
-    k_ref,
-    v_ref,
+    q_hbm,
+    k_hbm,
+    v_hbm,
     w_hbm,
     cot_hbm,
     mixed_hbm,
@@ -69,19 +68,22 @@
     dk_ref,
     dv_ref,
     dw_ref,
+    q_ref,
+    k_ref,
+    v_ref,
     w_ref,
     cot_ref,
     mixed_ref,
     win,
     co1,
     co2,
-    pair2,
     bias,
     go_t,
     att_t,
     keep,
     gsend,
     grecv,
+    piece_grad,
     rs_core_send,
     rs_core_recv,
     rs_x_send,
@@ -118,18 +120,28 @@
 
     sibling = (dp + 1 - 2 * core, me)
 
-    load_w = pltpu.make_async_copy(w_hbm, w_ref, load_sem.at[0])
-    load_cot = pltpu.make_async_copy(cot_hbm, cot_ref, load_sem.at[1])
-    load_w.start()
-    load_cot.start()
-
     barrier = pltpu.get_barrier_semaphore()
-    partners = [ctx(o) for o in (1, -1, 2, -2, 7, -7, 8, -8, 16)]
+    partners = [ctx(o) for o in (1, -1, 2, -2, 6, -6, 7, -7, 8, -8, 16)]
     partners += [row_peer(s) for s in range(1, 8)]
     partners += [(lax.rem(x + s, 4) * 2 + core, me) for s in range(1, 4)]
     partners += [sibling]
     for partner in partners:
         pl.semaphore_signal(barrier, inc=1, device_id=partner, device_id_type=MESH)
+
+    loads = [
+        pltpu.make_async_copy(source, target, load_sem.at[index])
+        for index, (source, target) in enumerate(
+            (
+                (k_hbm, k_ref),
+                (v_hbm, v_ref),
+                (q_hbm, q_ref),
+                (w_hbm, w_ref),
+                (cot_hbm, cot_ref),
+            )
+        )
+    ]
+    for load in loads:
+        load.start()
 
     half = pl.multiple_of(parity * 64, 64)
     other_half = pl.multiple_of(64 - parity * 64, 64)
@@ -139,13 +151,13 @@
     mean2 = (entry >= 128) & (lax.shift_right_logical(token, 2) == entry - 128)
     means = jnp.where(mean1, 0.5, jnp.where(mean2, 0.25, 0.0)).astype(BF16)
     for kv, source in enumerate((k_ref, v_ref)):
+        loads[kv].wait()
         coarse = dot(means, source[...], 1, 0).astype(BF16)
         for h in range(HEADS):
             cols = slice(h * HEAD_DIM, (h + 1) * HEAD_DIM)
             win[h, kv, OWN * BLOCK : (OWN + 2) * BLOCK, :] = source[:, cols]
             co1[h, kv] = coarse[:128, cols]
             co2[h, kv] = coarse[128:, cols]
-            pair2[h, kv, pl.ds(half, 64), :] = coarse[128:, cols]
 
     pl.semaphore_wait(barrier, len(partners))
 
@@ -186,25 +198,36 @@
     def returned(h, index):
         return grecv.at[h, index]
 
-    def first_sends(h):
-        piece = pair2.at[h, :, pl.ds(half, 64), :]
-        send(sems(h), R_PAIR, piece, piece, ctx(-tau), inner)
+    def send_level2(h):
+        piece = co2.at[h]
+        rows = pl.ds(pl.multiple_of(NEAR2 * BLOCK + half, 64), 64)
+        send(sems(h), R_NEAR2, piece, win.at[h, :, rows, :], ctx(7 * tau), outer)
+        send(sems(h), R_PAIR, piece, win.at[h, :, rows, :], ctx(6 * tau), inner)
+
+    def send_level1(h):
         send(sems(h), R_NEAR1, co1.at[h], window(h, NEAR1), ctx(2 * pi))
         send(sems(h), R_FAR1, co1.at[h], window(h, FAR1), ctx(-2 * pi))
+
+    def send_fine(h):
         send(sems(h), R_NEXT, window(h, OWN), window(h, NEXT), ctx(-1))
         send(sems(h), R_PREV, window(h, OWN + 1), window(h, PREV), ctx(1))
 
-    def relay_pair(h):
+    def relay_near(h):
         @pl.when(outer)
         def _():
-            arrive(sems(h), R_PAIR, pair2.at[h, :, pl.ds(other_half, 64), :], ctx(tau))
-
-        send(sems(h), R_NEAR2, pair2.at[h], window(h, NEAR2), ctx(7 * tau), outer)
-
-    def relay_near(h):
-        arrive(sems(h), R_NEAR2, window(h, NEAR2), ctx(tau))
+            first = pl.ds(pl.multiple_of(NEAR2 * BLOCK + other_half, 64), 64)
+            second = pl.ds(pl.multiple_of(NEAR2 * BLOCK + half, 64), 64)
+            arrive(sems(h), R_NEAR2, win.at[h, :, first, :], ctx(tau))
+            arrive(sems(h), R_PAIR, win.at[h, :, second, :], ctx(tau))
+
+        @pl.when(inner)
+        def _():
+            arrive(sems(h), R_NEAR2, window(h, NEAR2), ctx(tau))
+
         send(sems(h), R_NEAR2, window(h, NEAR2), window(h, NEAR2), ctx(tau), outer)
         send(sems(h), R_FAR2, window(h, NEAR2), window(h, FAR2), ctx(tau), inner)
+
+    def relay_third(h):
         arrive(sems(h), R_NEAR1, window(h, NEAR1), ctx(2 * pi))
         send(sems(h), R_THIRD1, window(h, NEAR1), window(h, THIRD1), ctx(pi))
 
@@ -282,25 +305,34 @@
     def outgoing(h, index):
         return gsend.at[h, :, slot(index), :]
 
-    def back_first(h):
+    def back_copy(h):
         send(sems(h), B_COPY2, outgoing(h, 4), returned(h, G_COPY2), ctx(8 * tau))
+
+    def back_pass(h):
         send(sems(h), B_THIRD1, outgoing(h, 3), returned(h, G_THIRD1), ctx(pi))
+
+    def back_level1(h):
         send(sems(h), B_FAR1, outgoing(h, 2), returned(h, G_FAR1), ctx(2 * pi))
+
+    def back_fine(h):
         send(sems(h), B_NEXT, outgoing(h, 0), returned(h, G_NEXT), ctx(-1))
         send(sems(h), B_PREV, outgoing(h, 1), returned(h, G_PREV), ctx(1))
 
     def back_far(h):
         arrive(sems(h), B_COPY2, returned(h, G_COPY2), ctx(-8 * tau))
+        own = keep[h, :, slot(1), :] + grecv[h, G_COPY2].astype(F32)
+        keep[h, :, slot(1), :] = own
 
         @pl.when(inner)
         def _():
             arrive(sems(h), B_FAR2, returned(h, G_FAR2), ctx(-tau))
-
-        theirs = grecv[h, G_COPY2].astype(F32)
-        more = jnp.where(inner, grecv[h, G_FAR2].astype(F32), 0.0)
-        gsend[h, :, slot(6), :] = (keep[h, :, slot(1), :] + theirs + more).astype(BF16)
+            keep[h, :, slot(1), :] = own + grecv[h, G_FAR2].astype(F32)
+
+        gsend[h, :, slot(6), :] = keep[h, :, slot(1), :].astype(BF16)
         send(sems(h), B_FAR2, outgoing(h, 6), returned(h, G_FAR2), ctx(tau), outer)
         send(sems(h), B_NEAR2, outgoing(h, 6), returned(h, G_NEAR2), ctx(tau), inner)
+
+    def back_third(h):
         arrive(sems(h), B_THIRD1, returned(h, G_THIRD1), ctx(pi))
         theirs = grecv[h, G_THIRD1].astype(F32)
         gsend[h, :, slot(5), :] = (keep[h, :, slot(0), :] + theirs).astype(BF16)
@@ -311,16 +343,10 @@
         theirs = grecv[h, G_NEAR2].astype(F32)
         gsend[h, :, slot(7), :] = (keep[h, :, slot(2), :] + theirs).astype(BF16)
         send(sems(h), B_NEAR2, outgoing(h, 7), returned(h, G_NEAR2), ctx(-tau), inner)
-        send(sems(h), B_PAIR, outgoing(h, 7), returned(h, G_PAIR), ctx(7 * tau), outer)
-
-    def back_pair(h):
-        @pl.when(outer)
-        def _():
-            arrive(sems(h), B_PAIR, returned(h, G_PAIR), ctx(7 * tau))
-
-        theirs = grecv.at[h, G_PAIR, :, pl.ds(other_half, 64), :]
-        mine = grecv.at[h, G_PIECE, :, pl.ds(0, 64), :]
-        send(sems(h), B_PIECE, theirs, mine, ctx(tau), outer)
+        first = pl.ds(pl.multiple_of(7 * BLOCK + other_half, 64), 64)
+        second = pl.ds(pl.multiple_of(7 * BLOCK + half, 64), 64)
+        send(sems(h), B_PIECE, gsend.at[h, :, first, :], piece_grad.at[h], ctx(7 * tau), outer)
+        send(sems(h), B_PIECE, gsend.at[h, :, second, :], piece_grad.at[h], ctx(6 * tau), outer)
 
     def finish(h):
         cols = slice(h * HEAD_DIM, (h + 1) * HEAD_DIM)
@@ -328,16 +354,10 @@
         arrive(sems(h), B_PREV, returned(h, G_PREV), ctx(-1))
         arrive(sems(h), B_FAR1, returned(h, G_FAR1), ctx(-2 * pi))
         arrive(sems(h), B_NEAR1, returned(h, G_NEAR1), ctx(2 * pi))
-
-        @pl.when(inner)
-        def _():
-            arrive(sems(h), B_PIECE, grecv.at[h, G_PIECE, :, pl.ds(0, 64), :], ctx(-tau))
-
+        arrive(sems(h), B_PIECE, piece_grad.at[h], ctx(7 * tau))
         for kv, own in enumerate((dk_ref, dv_ref)):
             level1 = grecv[h, G_FAR1, kv].astype(F32) + grecv[h, G_NEAR1, kv].astype(F32)
-            pair = grecv[h, G_PAIR, kv, pl.ds(half, 64), :]
-            level2 = jnp.where(outer, pair, grecv[h, G_PIECE, kv, :64, :])
-            entries = jnp.concatenate([level1.astype(BF16), level2], axis=0)
+            entries = jnp.concatenate([level1.astype(BF16), piece_grad[h, kv]], axis=0)
             spread = dot(means, entries, 0, 0)
             own[:BLOCK, cols] += spread[:BLOCK] + grecv[h, G_PREV, kv].astype(F32)
             own[BLOCK:, cols] += spread[BLOCK:] + grecv[h, G_NEXT, kv].astype(F32)
@@ -398,62 +418,86 @@
             total = total + rs_z_recv[step - 1]
         dw_ref[...] = total
 
-    for h in range(HEADS):
-        first_sends(h)
+    send_level2(0)
+    send_level2(1)
+    send_level2(2)
+    send_level2(3)
+    send_level1(0)
+    send_level1(1)
+    send_level1(2)
+    send_level1(3)
+    send_fine(0)
+    send_fine(1)
+    send_fine(2)
+    send_fine(3)
     masks()
-    load_w.wait()
-    load_cot.wait()
+    for load in loads[2:]:
+        load.wait()
     go_t[...] = dot(w_ref[...], cot_ref[...], 1, 1).astype(BF16)
-    for h in range(HEADS):
-        relay_pair(h)
     relay_near(0)
     relay_near(1)
+    relay_near(2)
+    relay_near(3)
     relay_far(0)
+    relay_far(1)
+    relay_far(2)
+    relay_far(3)
+    relay_third(0)
+    relay_third(1)
+    relay_third(2)
+    relay_third(3)
     last_arrivals(0)
     attend(0)
-    back_first(0)
-    weight_core(0)
-    relay_near(2)
-    relay_far(1)
+    back_copy(0)
+    back_pass(0)
+    back_level1(0)
     last_arrivals(1)
     attend(1)
-    back_first(1)
-    weight_core(1)
-    relay_near(3)
-    relay_far(2)
+    back_copy(1)
+    back_pass(1)
+    back_level1(1)
     back_far(0)
-    weight_x(0)
     last_arrivals(2)
     attend(2)
-    back_first(2)
-    weight_core(2)
-    relay_far(3)
+    back_copy(2)
+    back_pass(2)
+    back_level1(2)
     back_far(1)
-    back_near(0)
-    weight_x(1)
     last_arrivals(3)
     attend(3)
-    back_first(3)
+    back_copy(3)
+    back_pass(3)
+    back_level1(3)
+    back_far(2)
+    back_near(0)
+    weight_core(0)
+    weight_core(1)
+    weight_core(2)
     weight_core(3)
-    back_far(2)
+    back_far(3)
     back_near(1)
-    back_pair(0)
+    back_fine(0)
+    weight_x(0)
+    weight_x(1)
     weight_x(2)
     weight_x(3)
+    back_near(2)
+    back_fine(1)
+    back_fine(2)
+    back_fine(3)
+    back_third(0)
+    back_third(1)
+    back_third(2)
+    back_third(3)
+    back_near(3)
     for part in range(4):
         cols = slice(part * 512, (part + 1) * 512)
         mixed_ref[:, cols] = dot(att_t[...], w_ref[:, cols], 0, 0).astype(BF16)
-    store = pltpu.make_async_copy(mixed_ref, mixed_hbm, load_sem.at[2])
+    store = pltpu.make_async_copy(mixed_ref, mixed_hbm, load_sem.at[5])
     store.start()
-    back_far(3)
-    back_near(2)
-    back_pair(1)
     weight_y()
-    back_near(3)
-    back_pair(2)
     weight_z()
     finish(0)
-    back_pair(3)
     finish(1)
     finish(2)
     weight_end()
@@ -467,6 +511,31 @@
 
 
 SENDS = 112
+
+
+def hand_over(*refs):
+    sources, targets, buffers, in_sems, out_sems = refs[:5], refs[5:10], refs[10:15], refs[15], refs[16]
+    stages = []
+    for i in range(5):
+        rows = sources[i].shape[0]
+        parts = 1 if i == 4 else 4 if i == 0 else 2
+        for part in range(parts):
+            size = rows // parts
+            span = pl.ds(part * size, size)
+            n = len(stages)
+            stages.append(
+                (
+                    pltpu.make_async_copy(sources[i].at[span], buffers[i].at[span], in_sems.at[n]),
+                    pltpu.make_async_copy(buffers[i].at[span], targets[i].at[span], out_sems.at[n]),
+                )
+            )
+    for fetch, _ in stages:
+        fetch.start()
+    for fetch, store in stages:
+        fetch.wait()
+        store.start()
+    for _, store in stages:
+        store.wait()
 
 
 def shards(queries, keys, values, out_weight, cotangent, prefix):
@@ -482,22 +551,25 @@
             jax.ShapeDtypeStruct((TOK, HD), F32),
             jax.ShapeDtypeStruct((2, D), F32),
         ),
-        in_specs=[pl.BlockSpec(memory_space=pltpu.SMEM), vmem, vmem, vmem, anywhere, anywhere],
+        in_specs=[pl.BlockSpec(memory_space=pltpu.SMEM)] + [anywhere] * 5,
         out_specs=(anywhere, vmem, vmem, vmem, vmem),
         scratch_shapes=[
+            pltpu.VMEM((TOK, HD), BF16),
+            pltpu.VMEM((TOK, HD), BF16),
+            pltpu.VMEM((TOK, HD), BF16),
             pltpu.VMEM((HD, D), BF16),
             pltpu.VMEM((TOK, D), BF16),
             pltpu.VMEM((TOK, D), BF16),
             pltpu.VMEM(pair + (KEYS, HEAD_DIM), BF16),
             pltpu.VMEM(pair + (128, HEAD_DIM), BF16),
             pltpu.VMEM(pair + (64, HEAD_DIM), BF16),
-            pltpu.VMEM(pair + (128, HEAD_DIM), BF16),
             pltpu.VMEM((KEYS, TOK), F32),
             pltpu.VMEM((HD, TOK), BF16),
             pltpu.VMEM((HD, TOK), BF16),
             pltpu.VMEM(pair + (3 * BLOCK, HEAD_DIM), F32),
             pltpu.VMEM(pair + (8 * BLOCK, HEAD_DIM), BF16),
-            pltpu.VMEM((HEADS, 10, 2, BLOCK, HEAD_DIM), BF16),
+            pltpu.VMEM((HEADS, 8, 2, BLOCK, HEAD_DIM), BF16),
+            pltpu.VMEM(pair + (64, HEAD_DIM), BF16),
             pltpu.VMEM((HEADS, 64, D), BF16),
             pltpu.VMEM((HEADS, 64, D), BF16),
             pltpu.VMEM((HEADS, 64, D), BF16),
@@ -507,7 +579,7 @@
             pltpu.VMEM((3, 16, D), BF16),
             pltpu.VMEM((8, 2, D), F32),
             pltpu.VMEM((7, 2, D), F32),
-            pltpu.SemaphoreType.DMA((3,)),
+            pltpu.SemaphoreType.DMA((6,)),
             pltpu.SemaphoreType.DMA((SENDS,)),
             pltpu.SemaphoreType.DMA((HEADS, KINDS)),
             pltpu.SemaphoreType.DMA((13,)),
@@ -520,6 +592,16 @@
         ),
         name="hier_attention",
     )(prefix, queries[0], keys[0], values[0], out_weight, cotangent[0])
+    results = (mixed, dq, dk, dv, dw)
+    mixed, dq, dk, dv, dw = pl.pallas_call(
+        hand_over,
+        out_shape=tuple(jax.ShapeDtypeStruct(a.shape, a.dtype) for a in results),
+        in_specs=[anywhere] * 5,
+        out_specs=(anywhere,) * 5,
+        scratch_shapes=[pltpu.VMEM(a.shape, a.dtype) for a in results]
+        + [pltpu.SemaphoreType.DMA((11,)), pltpu.SemaphoreType.DMA((11,))],
+        name="hand_over",
+    )(*results)
     return mixed[None], dq[None], dk[None], dv[None], dw
 
 

time: 139 us -> 101 us (0.73); the launches traced: 137 us -> 100 us
  Pallas kernels: 130 us -> 99.1 us
  local copies, waits for them, and re-layouts: 5.42 us -> 0 us
    pallas_call x1, Pallas kernels: 130 us -> 96.5 us  [shards(): pl.pallas_call(kernel, out_shape=(jax.ShapeDtypeStruct((TOK, D), BF16), j...]
    unnamed x13 -> x0, local copies, waits for them, and re-layouts: 5.42 us -> none
    pallas_call x0 -> x1, Pallas kernels: none -> 2.62 us  [shards(): pl.pallas_call(hand_over, out_shape=tuple((jax.ShapeDtypeStruct(a.shape,...]
where the time goes in v2:
time: 101 us; the launch traced here: 100 us
  Pallas kernels  99.1 us (98%)
  between operations  1.29 us (1%)
    pallas_call x1, Pallas kernels, shards(): pl.pallas_call(kernel, out_shape=(jax.ShapeDtypeStruct((TOK, D), BF16), j...  96.5 us
    pallas_call x1, Pallas kernels, shards(): pl.pallas_call(hand_over, out_shape=tuple((jax.ShapeDtypeStruct(a.shape,...  2.62 us

profile of v2, /device:TPU:2, one launch (start us, length us, event | category | flops | bytes accessed | tf_op | source)
XLA Modules:
  0.0 100.4 jit_solution(7694973679394724874)
XLA Ops:
  1.3 96.5 %hier_attention.1 = (bf16[256,2048]{1,0:T(8,128)(2,1)}, f32[256,512]{1,0:T(8,128)}, f32[256,512]{1,0:T(8,128)}, f32[256,512]{1,0:T(8,128)}, f32[2,2048]{1,0:T(2,128)}) custom-call(s32[1]{0:T(128)S(6)} %copy.11.prefix_ref, bf16[256,512]{1,0:T(8,128)(2,1)} %bitcast.13, bf16[256,512]{1,0:T(8,128)(2,1)} %bitcast.14, bf16[256,512]{1,0:T(8,128)(2,1)} %bitcast.15, ...), custom_call_target="tpu_custom_call" | custom-call | flops 3700000000 | bytes 8000000 | tf_op jit(solution)/shard_map/hier_attention/pallas_call | solution.py:545
  97.8 2.6 %hand_over.1 = (bf16[256,2048]{1,0:T(8,128)(2,1)}, f32[256,512]{1,0:T(8,128)}, f32[256,512]{1,0:T(8,128)}, f32[256,512]{1,0:T(8,128)}, f32[2,2048]{1,0:T(2,128)}) custom-call(bf16[256,2048]{1,0:T(8,128)(2,1)} %get-tuple-element.15.refs_0_, f32[256,512]{1,0:T(8,128)} %get-tuple-element.16.refs_1_, f32[256,512]{1,0:T(8,128)} %get-tuple-element.17.refs_2_, ...), custom_call_target="tpu_custom_call" | custom-call | tf_op jit(solution)/shard_map/hand_over/pallas_call | solution.py:596

commit v3 on v2

--- a/solution.py
+++ b/solution.py
@@ -14,6 +14,7 @@
 LEN = 8192
 CTX = 32
 KEYS = 1280
+WIDE = D // 2
 SCALE = HEAD_DIM**-0.5
 LOG2E = 1.4426950408889634
 DEAD = -1e30
@@ -84,13 +85,19 @@
     gsend,
     grecv,
     piece_grad,
+    rs_part,
     rs_core_send,
     rs_core_recv,
-    rs_x_send,
-    rs_x_recv,
-    rs_own,
-    rs_y_send,
-    rs_y_recv,
+    rs_left,
+    rs_right,
+    rs_left_x,
+    rs_left_own,
+    rs_left_send,
+    rs_left_y,
+    rs_right_y,
+    rs_right_own,
+    rs_right_send,
+    rs_right_x,
     rs_z_send,
     rs_z_recv,
     load_sem,
@@ -362,57 +369,83 @@
             own[:BLOCK, cols] += spread[:BLOCK] + grecv[h, G_PREV, kv].astype(F32)
             own[BLOCK:, cols] += spread[BLOCK:] + grecv[h, G_NEXT, kv].astype(F32)
 
-    def weight_part(h, which):
-        rows = pl.ds(pl.multiple_of(h * HEAD_DIM + which * 64, 64), 64)
-        return dot(att_t[rows, :], cot_ref[...], 1, 0)
-
     def weight_core(h):
-        rs_core_send[h] = weight_part(h, 1 - core).astype(BF16)
+        theirs = pl.ds(pl.multiple_of(h * HEAD_DIM + (1 - core) * 64, 64), 64)
+        ours = pl.ds(pl.multiple_of(h * HEAD_DIM + core * 64, 64), 64)
+        rows = jnp.concatenate([att_t[theirs, :], att_t[ours, :]], axis=0)
+        part = dot(rows, cot_ref[...], 1, 0)
+        rs_core_send[h] = part[:64].astype(BF16)
+        rs_part[h] = part[64:]
         send(sems(h), W_CORE, rs_core_send.at[h], rs_core_recv.at[h], sibling)
 
     rs_sems = (send_sem, rs_recv_sem)
 
-    def weight_x(h):
+    def weight_first(h):
         arrive(sems(h), W_CORE, rs_core_recv.at[h], sibling)
-        total = weight_part(h, core) + rs_core_recv[h].astype(F32)
-        rs_x_send[h] = total.astype(BF16)
-
-        @pl.when(x == h)
-        def _():
-            rs_own[...] = total
-
-        step = lax.rem(x - h + 4, 4)
-        place = jnp.maximum(step - 1, 0)
-        send(rs_sems, place, rs_x_send.at[h], rs_x_recv.at[place], (h * 2 + core, me), x != h)
-
-    def weight_y():
+        total = rs_part[h] + rs_core_recv[h].astype(F32)
+        rs_part[h] = total
+        rs_left[h] = total[:, :WIDE].astype(BF16)
+        rs_right[h] = total[:, WIDE:].astype(BF16)
+        place = jnp.maximum(lax.rem(x - h + 4, 4) - 1, 0)
+        device = (h * 2 + core, me)
+        send(rs_sems, place, rs_left.at[h], rs_left_x.at[place], device, x != h)
+        if h % 2 == 1:
+            for step in range(1, 4):
+                rows = pl.ds(pl.multiple_of(lax.rem(y + step, 4) * 16, 16), 16)
+                pair = pl.ds(h - 1, 2)
+                source = rs_right.at[pair, rows, :]
+                target = rs_right_y.at[step - 1, pair]
+                send(rs_sems, 3 * (h // 2) + 2 + step, source, target, column_peer(step))
+
+    def weight_left():
         for step in range(1, 4):
             device = (lax.rem(x + step, 4) * 2 + core, me)
-            arrive(rs_sems, step - 1, rs_x_recv.at[step - 1], device)
-        total = rs_own[...]
+            arrive(rs_sems, step - 1, rs_left_x.at[step - 1], device)
+        total = rs_part[x, :, :WIDE]
         for step in range(1, 4):
-            total = total + rs_x_recv[step - 1].astype(F32)
-        rs_own[...] = total
-        rs_y_send[...] = total.astype(BF16)
+            total = total + rs_left_x[step - 1].astype(F32)
+        rs_left_own[...] = total
+        rs_left_send[...] = total.astype(BF16)
         for step in range(1, 4):
             rows = pl.ds(pl.multiple_of(lax.rem(y + step, 4) * 16, 16), 16)
-            send(rs_sems, 2 + step, rs_y_send.at[rows], rs_y_recv.at[step - 1], column_peer(step))
+            source = rs_left_send.at[rows]
+            send(rs_sems, 10 + step, source, rs_left_y.at[step - 1], column_peer(step))
+
+    def weight_right():
+        for h in (1, 3):
+            for step in range(1, 4):
+                part = rs_right_y.at[step - 1, pl.ds(h - 1, 2)]
+                arrive(rs_sems, 3 * (h // 2) + 2 + step, part, column_peer(step))
+        total = rs_part[:, pl.ds(pl.multiple_of(y * 16, 16), 16), WIDE:]
+        for step in range(1, 4):
+            total = total + rs_right_y[step - 1].astype(F32)
+        rs_right_own[...] = total
+        rs_right_send[...] = total.astype(BF16)
+        for step in range(1, 4):
+            head = lax.rem(x + step, 4)
+            device = (head * 2 + core, me)
+            send(rs_sems, 13 + step, rs_right_send.at[head], rs_right_x.at[step - 1], device)
 
     def weight_z():
+        left = rs_left_own[pl.ds(pl.multiple_of(y * 16, 16), 16), :]
+        right = rs_right_own[x]
         for step in range(1, 4):
-            arrive(rs_sems, 2 + step, rs_y_recv.at[step - 1], column_peer(step))
-        total = rs_own[pl.ds(pl.multiple_of(y * 16, 16), 16), :]
+            arrive(rs_sems, 10 + step, rs_left_y.at[step - 1], column_peer(step))
+            device = (lax.rem(x + step, 4) * 2 + core, me)
+            arrive(rs_sems, 13 + step, rs_right_x.at[step - 1], device)
         for step in range(1, 4):
-            total = total + rs_y_recv[step - 1].astype(F32)
+            left = left + rs_left_y[step - 1].astype(F32)
+            right = right + rs_right_x[step - 1].astype(F32)
         for part in range(8):
-            rs_z_send[part] = total[2 * part : 2 * part + 2]
+            rs_z_send[part, :, :WIDE] = left[2 * part : 2 * part + 2]
+            rs_z_send[part, :, WIDE:] = right[2 * part : 2 * part + 2]
         for step in range(1, 8):
             part = rs_z_send.at[lax.rem(z + step, 8)]
-            send(rs_sems, 5 + step, part, rs_z_recv.at[step - 1], row_peer(step))
+            send(rs_sems, 16 + step, part, rs_z_recv.at[step - 1], row_peer(step))
 
     def weight_end():
         for step in range(1, 8):
-            arrive(rs_sems, 5 + step, rs_z_recv.at[step - 1], row_peer(step))
+            arrive(rs_sems, 16 + step, rs_z_recv.at[step - 1], row_peer(step))
         total = rs_z_send[z]
         for step in range(1, 8):
             total = total + rs_z_recv[step - 1]
@@ -425,11 +458,10 @@
     send_level1(0)
     send_level1(1)
     send_level1(2)
-    send_level1(3)
     send_fine(0)
     send_fine(1)
     send_fine(2)
-    send_fine(3)
+    send_level1(3)
     masks()
     for load in loads[2:]:
         load.wait()
@@ -441,46 +473,47 @@
     relay_far(0)
     relay_far(1)
     relay_far(2)
-    relay_far(3)
+    send_fine(3)
     relay_third(0)
     relay_third(1)
     relay_third(2)
-    relay_third(3)
     last_arrivals(0)
     attend(0)
     back_copy(0)
     back_pass(0)
-    back_level1(0)
     last_arrivals(1)
     attend(1)
     back_copy(1)
     back_pass(1)
-    back_level1(1)
+    relay_far(3)
+    relay_third(3)
+    back_level1(0)
     back_far(0)
     last_arrivals(2)
     attend(2)
     back_copy(2)
     back_pass(2)
-    back_level1(2)
+    back_level1(1)
     back_far(1)
     last_arrivals(3)
     attend(3)
     back_copy(3)
     back_pass(3)
-    back_level1(3)
-    back_far(2)
-    back_near(0)
+    back_level1(2)
     weight_core(0)
     weight_core(1)
     weight_core(2)
     weight_core(3)
+    back_level1(3)
+    back_far(2)
+    back_near(0)
     back_far(3)
+    weight_first(0)
+    weight_first(1)
+    weight_first(2)
+    weight_first(3)
     back_near(1)
     back_fine(0)
-    weight_x(0)
-    weight_x(1)
-    weight_x(2)
-    weight_x(3)
     back_near(2)
     back_fine(1)
     back_fine(2)
@@ -489,14 +522,15 @@
     back_third(1)
     back_third(2)
     back_third(3)
+    weight_left()
+    weight_right()
     back_near(3)
+    weight_z()
     for part in range(4):
         cols = slice(part * 512, (part + 1) * 512)
         mixed_ref[:, cols] = dot(att_t[...], w_ref[:, cols], 0, 0).astype(BF16)
     store = pltpu.make_async_copy(mixed_ref, mixed_hbm, load_sem.at[5])
     store.start()
-    weight_y()
-    weight_z()
     finish(0)
     finish(1)
     finish(2)
@@ -510,7 +544,7 @@
             pl.when(when)(copy.wait_send)
 
 
-SENDS = 112
+SENDS = 128
 
 
 def hand_over(*refs):
@@ -570,19 +604,25 @@
             pltpu.VMEM(pair + (8 * BLOCK, HEAD_DIM), BF16),
             pltpu.VMEM((HEADS, 8, 2, BLOCK, HEAD_DIM), BF16),
             pltpu.VMEM(pair + (64, HEAD_DIM), BF16),
+            pltpu.VMEM((HEADS, 64, D), F32),
             pltpu.VMEM((HEADS, 64, D), BF16),
             pltpu.VMEM((HEADS, 64, D), BF16),
-            pltpu.VMEM((HEADS, 64, D), BF16),
-            pltpu.VMEM((3, 64, D), BF16),
-            pltpu.VMEM((64, D), F32),
-            pltpu.VMEM((64, D), BF16),
-            pltpu.VMEM((3, 16, D), BF16),
+            pltpu.VMEM((HEADS, 64, WIDE), BF16),
+            pltpu.VMEM((HEADS, 64, WIDE), BF16),
+            pltpu.VMEM((3, 64, WIDE), BF16),
+            pltpu.VMEM((64, WIDE), F32),
+            pltpu.VMEM((64, WIDE), BF16),
+            pltpu.VMEM((3, 16, WIDE), BF16),
+            pltpu.VMEM((3, HEADS, 16, WIDE), BF16),
+            pltpu.VMEM((HEADS, 16, WIDE), F32),
+            pltpu.VMEM((HEADS, 16, WIDE), BF16),
+            pltpu.VMEM((3, 16, WIDE), BF16),
             pltpu.VMEM((8, 2, D), F32),
             pltpu.VMEM((7, 2, D), F32),
             pltpu.SemaphoreType.DMA((6,)),
             pltpu.SemaphoreType.DMA((SENDS,)),
             pltpu.SemaphoreType.DMA((HEADS, KINDS)),
-            pltpu.SemaphoreType.DMA((13,)),
+            pltpu.SemaphoreType.DMA((24,)),
         ],
         compiler_params=pltpu.CompilerParams(
             collective_id=0, has_side_effects=True, vmem_limit_bytes=56 << 20

time: 101 us -> 97 us (0.960)
  Pallas kernels: 99.1 us -> 95.5 us
    pallas_call x1, Pallas kernels: 96.5 us -> 92.8 us  [shards(): pl.pallas_call(kernel, out_shape=(jax.ShapeDtypeStruct((TOK, D), BF16), j...]
where the time goes in v3:
time: 97 us; the launch traced here: 96.9 us
  Pallas kernels  95.5 us (98%)
  between operations  1.45 us (1%)
    pallas_call x1, Pallas kernels, shards(): pl.pallas_call(kernel, out_shape=(jax.ShapeDtypeStruct((TOK, D), BF16), j...  92.8 us
    pallas_call x1, Pallas kernels, shards(): pl.pallas_call(hand_over, out_shape=tuple((jax.ShapeDtypeStruct(a.shape,...  2.62 us

profile of v3, /device:TPU:2, one launch (start us, length us, event | category | flops | bytes accessed | tf_op | source)
XLA Modules:
  0.0 96.9 jit_solution(18290268007433876288)
XLA Ops:
  1.3 92.8 %hier_attention.1 = (bf16[256,2048]{1,0:T(8,128)(2,1)}, f32[256,512]{1,0:T(8,128)}, f32[256,512]{1,0:T(8,128)}, f32[256,512]{1,0:T(8,128)}, f32[2,2048]{1,0:T(2,128)}) custom-call(s32[1]{0:T(128)S(6)} %copy.11.prefix_ref, bf16[256,512]{1,0:T(8,128)(2,1)} %bitcast.13, bf16[256,512]{1,0:T(8,128)(2,1)} %bitcast.14, bf16[256,512]{1,0:T(8,128)(2,1)} %bitcast.15, ...), custom_call_target="tpu_custom_call" | custom-call | flops 3700000000 | bytes 8000000 | tf_op jit(solution)/shard_map/hier_attention/pallas_call | solution.py:579
  94.1 2.6 %hand_over.1 = (bf16[256,2048]{1,0:T(8,128)(2,1)}, f32[256,512]{1,0:T(8,128)}, f32[256,512]{1,0:T(8,128)}, f32[256,512]{1,0:T(8,128)}, f32[2,2048]{1,0:T(2,128)}) custom-call(bf16[256,2048]{1,0:T(8,128)(2,1)} %get-tuple-element.15.refs_0_, f32[256,512]{1,0:T(8,128)} %get-tuple-element.16.refs_1_, f32[256,512]{1,0:T(8,128)} %get-tuple-element.17.refs_2_, ...), custom_call_target="tpu_custom_call" | custom-call | tf_op jit(solution)/shard_map/hand_over/pallas_call | solution.py:636

commit v4 on v3

--- a/solution.py
+++ b/solution.py
@@ -127,14 +127,6 @@
 
     sibling = (dp + 1 - 2 * core, me)
 
-    barrier = pltpu.get_barrier_semaphore()
-    partners = [ctx(o) for o in (1, -1, 2, -2, 6, -6, 7, -7, 8, -8, 16)]
-    partners += [row_peer(s) for s in range(1, 8)]
-    partners += [(lax.rem(x + s, 4) * 2 + core, me) for s in range(1, 4)]
-    partners += [sibling]
-    for partner in partners:
-        pl.semaphore_signal(barrier, inc=1, device_id=partner, device_id_type=MESH)
-
     loads = [
         pltpu.make_async_copy(source, target, load_sem.at[index])
         for index, (source, target) in enumerate(
@@ -150,105 +142,13 @@
     for load in loads:
         load.start()
 
-    half = pl.multiple_of(parity * 64, 64)
-    other_half = pl.multiple_of(64 - parity * 64, 64)
-    entry = lax.broadcasted_iota(jnp.int32, (192, TOK), 0)
-    token = lax.broadcasted_iota(jnp.int32, (192, TOK), 1)
-    mean1 = (entry < 128) & (lax.shift_right_logical(token, 1) == entry)
-    mean2 = (entry >= 128) & (lax.shift_right_logical(token, 2) == entry - 128)
-    means = jnp.where(mean1, 0.5, jnp.where(mean2, 0.25, 0.0)).astype(BF16)
-    for kv, source in enumerate((k_ref, v_ref)):
-        loads[kv].wait()
-        coarse = dot(means, source[...], 1, 0).astype(BF16)
-        for h in range(HEADS):
-            cols = slice(h * HEAD_DIM, (h + 1) * HEAD_DIM)
-            win[h, kv, OWN * BLOCK : (OWN + 2) * BLOCK, :] = source[:, cols]
-            co1[h, kv] = coarse[:128, cols]
-            co2[h, kv] = coarse[128:, cols]
-
-    pl.semaphore_wait(barrier, len(partners))
-
-    started = []
-
-    def send(sems, kind, src, dst, device, when=None):
-        send_sems, recv_sems = sems
-        copy = pltpu.make_async_remote_copy(
-            src_ref=src,
-            dst_ref=dst,
-            send_sem=send_sems.at[len(started)],
-            recv_sem=recv_sems.at[kind],
-            device_id=device,
-            device_id_type=MESH,
-        )
-        if when is None:
-            copy.start()
-        else:
-            pl.when(when)(copy.start)
-        started.append((when, copy))
-
-    def arrive(sems, kind, dst, device):
-        pltpu.make_async_remote_copy(
-            src_ref=dst,
-            dst_ref=dst,
-            send_sem=sems[0].at[0],
-            recv_sem=sems[1].at[kind],
-            device_id=device,
-            device_id_type=MESH,
-        ).wait_recv()
-
-    def sems(h):
-        return send_sem, recv_sem.at[h]
-
-    def window(h, index):
-        return win.at[h, :, slot(index), :]
-
-    def returned(h, index):
-        return grecv.at[h, index]
-
-    def send_level2(h):
-        piece = co2.at[h]
-        rows = pl.ds(pl.multiple_of(NEAR2 * BLOCK + half, 64), 64)
-        send(sems(h), R_NEAR2, piece, win.at[h, :, rows, :], ctx(7 * tau), outer)
-        send(sems(h), R_PAIR, piece, win.at[h, :, rows, :], ctx(6 * tau), inner)
-
-    def send_level1(h):
-        send(sems(h), R_NEAR1, co1.at[h], window(h, NEAR1), ctx(2 * pi))
-        send(sems(h), R_FAR1, co1.at[h], window(h, FAR1), ctx(-2 * pi))
-
-    def send_fine(h):
-        send(sems(h), R_NEXT, window(h, OWN), window(h, NEXT), ctx(-1))
-        send(sems(h), R_PREV, window(h, OWN + 1), window(h, PREV), ctx(1))
-
-    def relay_near(h):
-        @pl.when(outer)
-        def _():
-            first = pl.ds(pl.multiple_of(NEAR2 * BLOCK + other_half, 64), 64)
-            second = pl.ds(pl.multiple_of(NEAR2 * BLOCK + half, 64), 64)
-            arrive(sems(h), R_NEAR2, win.at[h, :, first, :], ctx(tau))
-            arrive(sems(h), R_PAIR, win.at[h, :, second, :], ctx(tau))
-
-        @pl.when(inner)
-        def _():
-            arrive(sems(h), R_NEAR2, window(h, NEAR2), ctx(tau))
-
-        send(sems(h), R_NEAR2, window(h, NEAR2), window(h, NEAR2), ctx(tau), outer)
-        send(sems(h), R_FAR2, window(h, NEAR2), window(h, FAR2), ctx(tau), inner)
-
-    def relay_third(h):
-        arrive(sems(h), R_NEAR1, window(h, NEAR1), ctx(2 * pi))
-        send(sems(h), R_THIRD1, window(h, NEAR1), window(h, THIRD1), ctx(pi))
-
-    def relay_far(h):
-        arrive(sems(h), R_FAR2, window(h, FAR2), ctx(tau))
-        send(sems(h), R_FAR2, window(h, FAR2), window(h, FAR2), ctx(-tau), inner)
-        send(sems(h), R_COPY2, window(h, FAR2), window(h, COPY2), ctx(-8 * tau))
-
-    def last_arrivals(h):
-        arrive(sems(h), R_NEXT, window(h, NEXT), ctx(1))
-        arrive(sems(h), R_PREV, window(h, PREV), ctx(-1))
-        arrive(sems(h), R_FAR1, window(h, FAR1), ctx(2 * pi))
-        arrive(sems(h), R_THIRD1, window(h, THIRD1), ctx(pi))
-        arrive(sems(h), R_COPY2, window(h, COPY2), ctx(8 * tau))
+    barrier = pltpu.get_barrier_semaphore()
+    partners = [ctx(o) for o in (1, -1, 2, -2, 6, -6, 7, -7, 8, -8, 16)]
+    partners += [row_peer(s) for s in range(1, 8)]
+    partners += [(lax.rem(x + s, 4) * 2 + core, me) for s in range(1, 4)]
+    partners += [sibling]
+    for partner in partners:
+        pl.semaphore_signal(barrier, inc=1, device_id=partner, device_id_type=MESH)
 
     def masks():
         prefix_end = prefix_ref[0] * BLOCK
@@ -277,6 +177,108 @@
                 until = jnp.where(inside, prefix_end, 0)
                 usable = (place < before) | ((end <= until) & (end > 0))
                 bias[slot(index), :] = jnp.where(usable, float(level), DEAD)
+
+    masks()
+
+    half = pl.multiple_of(parity * 64, 64)
+    other_half = pl.multiple_of(64 - parity * 64, 64)
+    entry = lax.broadcasted_iota(jnp.int32, (192, TOK), 0)
+    token = lax.broadcasted_iota(jnp.int32, (192, TOK), 1)
+    mean1 = (entry < 128) & (lax.shift_right_logical(token, 1) == entry)
+    mean2 = (entry >= 128) & (lax.shift_right_logical(token, 2) == entry - 128)
+    means = jnp.where(mean1, 0.5, jnp.where(mean2, 0.25, 0.0)).astype(BF16)
+    for kv, source in enumerate((k_ref, v_ref)):
+        loads[kv].wait()
+        coarse = dot(means, source[...], 1, 0).astype(BF16)
+        for h in range(HEADS):
+            cols = slice(h * HEAD_DIM, (h + 1) * HEAD_DIM)
+            win[h, kv, OWN * BLOCK : (OWN + 2) * BLOCK, :] = source[:, cols]
+            co1[h, kv] = coarse[:128, cols]
+            co2[h, kv] = coarse[128:, cols]
+
+    pl.semaphore_wait(barrier, len(partners))
+
+    started = []
+
+    def send(sems, kind, src, dst, device, when=None):
+        send_sems, recv_sems = sems
+        copy = pltpu.make_async_remote_copy(
+            src_ref=src,
+            dst_ref=dst,
+            send_sem=send_sems.at[len(started)],
+            recv_sem=recv_sems.at[kind],
+            device_id=device,
+            device_id_type=MESH,
+        )
+        if when is None:
+            copy.start()
+        else:
+            pl.when(when)(copy.start)
+        started.append((when, copy))
+
+    def arrive(sems, kind, dst, device):
+        pltpu.make_async_remote_copy(
+            src_ref=dst,
+            dst_ref=dst,
+            send_sem=sems[0].at[0],
+            recv_sem=sems[1].at[kind],
+            device_id=device,
+            device_id_type=MESH,
+        ).wait_recv()
+
+    def sems(h):
+        return send_sem, recv_sem.at[h]
+
+    def window(h, index):
+        return win.at[h, :, slot(index), :]
+
+    def returned(h, index):
+        return grecv.at[h, index]
+
+    def send_level2(h):
+        piece = co2.at[h]
+        rows = pl.ds(pl.multiple_of(NEAR2 * BLOCK + half, 64), 64)
+        send(sems(h), R_NEAR2, piece, win.at[h, :, rows, :], ctx(7 * tau), outer)
+        send(sems(h), R_PAIR, piece, win.at[h, :, rows, :], ctx(6 * tau), inner)
+
+    def send_level1(h):
+        send(sems(h), R_NEAR1, co1.at[h], window(h, NEAR1), ctx(2 * pi))
+        send(sems(h), R_FAR1, co1.at[h], window(h, FAR1), ctx(-2 * pi))
+
+    def send_fine(h):
+        send(sems(h), R_NEXT, window(h, OWN), window(h, NEXT), ctx(-1))
+        send(sems(h), R_PREV, window(h, OWN + 1), window(h, PREV), ctx(1))
+
+    def relay_near(h):
+        @pl.when(outer)
+        def _():
+            first = pl.ds(pl.multiple_of(NEAR2 * BLOCK + other_half, 64), 64)
+            second = pl.ds(pl.multiple_of(NEAR2 * BLOCK + half, 64), 64)
+            arrive(sems(h), R_NEAR2, win.at[h, :, first, :], ctx(tau))
+            arrive(sems(h), R_PAIR, win.at[h, :, second, :], ctx(tau))
+
+        @pl.when(inner)
+        def _():
+            arrive(sems(h), R_NEAR2, window(h, NEAR2), ctx(tau))
+
+        send(sems(h), R_NEAR2, window(h, NEAR2), window(h, NEAR2), ctx(tau), outer)
+        send(sems(h), R_FAR2, window(h, NEAR2), window(h, FAR2), ctx(tau), inner)
+
+    def relay_third(h):
+        arrive(sems(h), R_NEAR1, window(h, NEAR1), ctx(2 * pi))
+        send(sems(h), R_THIRD1, window(h, NEAR1), window(h, THIRD1), ctx(pi))
+
+    def relay_far(h):
+        arrive(sems(h), R_FAR2, window(h, FAR2), ctx(tau))
+        send(sems(h), R_FAR2, window(h, FAR2), window(h, FAR2), ctx(-tau), inner)
+        send(sems(h), R_COPY2, window(h, FAR2), window(h, COPY2), ctx(-8 * tau))
+
+    def last_arrivals(h):
+        arrive(sems(h), R_NEXT, window(h, NEXT), ctx(1))
+        arrive(sems(h), R_PREV, window(h, PREV), ctx(-1))
+        arrive(sems(h), R_FAR1, window(h, FAR1), ctx(2 * pi))
+        arrive(sems(h), R_THIRD1, window(h, THIRD1), ctx(pi))
+        arrive(sems(h), R_COPY2, window(h, COPY2), ctx(8 * tau))
 
     def attend(h):
         cols = slice(h * HEAD_DIM, (h + 1) * HEAD_DIM)
@@ -462,7 +464,6 @@
     send_fine(1)
     send_fine(2)
     send_level1(3)
-    masks()
     for load in loads[2:]:
         load.wait()
     go_t[...] = dot(w_ref[...], cot_ref[...], 1, 1).astype(BF16)
@@ -526,16 +527,16 @@
     weight_right()
     back_near(3)
     weight_z()
+    finish(0)
+    finish(1)
+    finish(2)
+    finish(3)
     for part in range(4):
         cols = slice(part * 512, (part + 1) * 512)
         mixed_ref[:, cols] = dot(att_t[...], w_ref[:, cols], 0, 0).astype(BF16)
     store = pltpu.make_async_copy(mixed_ref, mixed_hbm, load_sem.at[5])
     store.start()
-    finish(0)
-    finish(1)
-    finish(2)
     weight_end()
-    finish(3)
     store.wait()
     for when, copy in started:
         if when is None:

time: 97 us -> 96.8 us (level)
  no operation moved by 1% of the time
where the time goes in v4:
time: 96.8 us; the launch traced here: 96.7 us
  Pallas kernels  95.2 us (98%)
  between operations  1.45 us (1%)
    pallas_call x1, Pallas kernels, shards(): pl.pallas_call(kernel, out_shape=(jax.ShapeDtypeStruct((TOK, D), BF16), j...  92.6 us
    pallas_call x1, Pallas kernels, shards(): pl.pallas_call(hand_over, out_shape=tuple((jax.ShapeDtypeStruct(a.shape,...  2.62 us

profile of v4, /device:TPU:2, one launch (start us, length us, event | category | flops | bytes accessed | tf_op | source)
XLA Modules:
  0.0 96.7 jit_solution(17741023159840533270)
XLA Ops:
  1.3 92.6 %hier_attention.1 = (bf16[256,2048]{1,0:T(8,128)(2,1)}, f32[256,512]{1,0:T(8,128)}, f32[256,512]{1,0:T(8,128)}, f32[256,512]{1,0:T(8,128)}, f32[2,2048]{1,0:T(2,128)}) custom-call(s32[1]{0:T(128)S(6)} %copy.11.prefix_ref, bf16[256,512]{1,0:T(8,128)(2,1)} %bitcast.13, bf16[256,512]{1,0:T(8,128)(2,1)} %bitcast.14, bf16[256,512]{1,0:T(8,128)(2,1)} %bitcast.15, ...), custom_call_target="tpu_custom_call" | custom-call | flops 3700000000 | bytes 8000000 | tf_op jit(solution)/shard_map/hier_attention/pallas_call | solution.py:580
  93.9 2.6 %hand_over.1 = (bf16[256,2048]{1,0:T(8,128)(2,1)}, f32[256,512]{1,0:T(8,128)}, f32[256,512]{1,0:T(8,128)}, f32[256,512]{1,0:T(8,128)}, f32[2,2048]{1,0:T(2,128)}) custom-call(bf16[256,2048]{1,0:T(8,128)(2,1)} %get-tuple-element.15.refs_0_, f32[256,512]{1,0:T(8,128)} %get-tuple-element.16.refs_1_, f32[256,512]{1,0:T(8,128)} %get-tuple-element.17.refs_2_, ...), custom_call_target="tpu_custom_call" | custom-call | tf_op jit(solution)/shard_map/hand_over/pallas_call | solution.py:637
